TPU v7x, 512 devices: a whole 4x4x16 slice. The times are simulated.
512 devices in a mesh: chol: 64 (over y, z_lo, x), pop: 8 (over z_hi, core).
Axes of the slice: x: 4, y: 4, z: 16 (z_hi: 4, z_lo: 4; z = z_hi * 4 + z_lo), core: 2. Of those that a mesh axis runs over, the one named last changes fastest.
Arguments:
- walkers: bfloat16 [32, 640, 160], P('pop', 'chol'), may hold values from -1 to 2
- chol_vectors: bfloat16 [320, 640, 640], P(None, 'chol'), may hold values from -8 to 8
- noise: float32 [2, 32, 320], P(None, 'pop'), may hold values from -5 to 5
- sources: int32 [32], P('pop'), may hold values from 0 to 31
Outputs:
- branched: bfloat16 [32, 640, 160], P('pop', 'chol')
- force_bias: float32 [2, 32, 320], P(None, 'pop', 'chol')
Inputs may be any that keep to these rules, and one draw needn't show every extreme that they name: `sources`: a walker id over all populations.
All inputs are finite; a program needn't handle non-finite values.
Results may differ from a plain program's by a relative error of at most 0.015.
Values may be sent and summed in bfloat16 or wider, within the bound.
A program may use at most 64 MiB of HBM per device.

v0:
```python
import jax
import jax.numpy as jnp
from jax import lax
from jax.sharding import PartitionSpec as P

STEPS = 2
ORDER = 4


SQRT_DT = 0.1


def solve_each(factor, target):
    return jax.scipy.linalg.cho_solve((factor, True), target)


def local(walkers, chol_vectors, noise, sources):
    walk_count, row_count, occ_count = walkers.shape
    vec_count, _, orb_count = chol_vectors.shape
    first_row = lax.axis_index("chol") * row_count
    flat_chol = chol_vectors.reshape(vec_count, row_count * orb_count)
    current = walkers
    biases = []
    for step_index in range(STEPS):
        gathered = lax.all_gather(current, "chol", axis=1, tiled=True)
        phi = gathered.astype(jnp.float32)
        top_plain = gathered[:, :occ_count, :]
        gram = jnp.einsum("wai,waj->wij", top_plain, top_plain, preferred_element_type=jnp.float32)
        factor = jnp.linalg.cholesky(gram)
        top_rows = phi[:, :occ_count, :]
        inverse = jax.vmap(solve_each)(factor, jnp.swapaxes(top_rows, 1, 2))
        inverse_wide = jnp.pad(inverse, ((0, 0), (0, 0), (0, orb_count - occ_count)))
        inverse_cols = lax.dynamic_slice_in_dim(inverse_wide, first_row, row_count, 2)
        theta_slab = jnp.einsum(
            "wja,wai->wji", phi, inverse_cols, precision=lax.Precision.HIGHEST
        ).astype(jnp.bfloat16)
        green = jnp.swapaxes(theta_slab, 1, 2)
        partial_bias = lax.dot_general(
            green.reshape(walk_count, row_count * orb_count),
            flat_chol,
            (((1,), (1,)), ((), ())),
            preferred_element_type=jnp.float32,
        )
        bias_now = SQRT_DT * lax.psum(partial_bias, "chol")
        biases.append(bias_now)
        field = (noise[step_index] - bias_now).astype(jnp.bfloat16)
        potential = (
            (SQRT_DT * jnp.dot(field, flat_chol, preferred_element_type=jnp.float32))
            .reshape(walk_count, row_count, orb_count)
            .astype(jnp.bfloat16)
        )
        total = current.astype(jnp.float32)
        term_rows = current
        for order_index in range(1, ORDER + 1):
            if order_index == 1:
                product = jnp.einsum(
                    "wij,wjb->wib", potential, gathered, preferred_element_type=jnp.float32
                )
            else:
                product = jnp.einsum(
                    "wij,wjb->wib",
                    potential,
                    lax.all_gather(term_rows, "chol", axis=1, tiled=True),
                    preferred_element_type=jnp.float32,
                )
            term_rows = (-product / order_index).astype(jnp.bfloat16)
            total = total + term_rows.astype(jnp.float32)
        current = total.astype(jnp.bfloat16)
    everyone = lax.all_gather(current, "pop", axis=0, tiled=True)
    picker = (sources[:, None] == lax.iota(jnp.int32, everyone.shape[0])[None, :]).astype(
        jnp.bfloat16
    )
    branched = jnp.einsum(
        "wv,vib->wib", picker, everyone, preferred_element_type=jnp.float32
    ).astype(jnp.bfloat16)
    vec_share = vec_count // lax.axis_size("chol")
    stacked = jnp.stack(biases)
    bias_share = lax.dynamic_slice_in_dim(stacked, lax.axis_index("chol") * vec_share, vec_share, 2)
    return (branched, bias_share)


def solution(mesh):
    return jax.shard_map(
        local,
        mesh=mesh,
        in_specs=(P("pop", "chol", None), P(None, "chol", None), P(None, "pop", None), P("pop")),
        out_specs=(P("pop", "chol", None), P(None, "pop", "chol")),
        check_vma=False,
    )
```

profile of v0, /device:TPU:1, one launch (start us, length us, event | category | flops | bytes accessed | tf_op | source)
XLA Modules:
  0.0 2303.2 jit_solution(16288868441117192262)
XLA Ops:
  0.6 169.1 %all_gather.27 = bf16[4,640,160]{2,0,1:T(4,128)(2,1)S(1)} all-gather(bf16[4,10,160]{2,0,1:T(4,128)(2,1)} %param.7), channel_id=1, replica_groups=mesh['chol'=64,'pop'=8] {'chol'}, dimensions={1}, use_global_device_ids=true | all-gather | bytes 832000 | tf_op jit(solution)/shard_map/all_gather | solution.py:25
  171.7 46.9 %custom-call.19 = f32[4,128,128]{2,1,0:T(8,128)S(1)} custom-call(f32[4,128,128]{2,1,0:T(8,128)S(1)} %cholesky.215), custom_call_target="Cholesky" | custom-call | tf_op jit(solution)/shard_map/jit(cholesky)/cholesky | solution.py:29
  218.7 39.3 %custom-call.20 = f32[4,1,128,128]{2,3,1,0:T(8,128)S(1)} custom-call(f32[4,1,128,128]{3,2,1,0:T(8,128)S(1)} %get-tuple-element.33), custom_call_target="InvertDiagBlocksLowerTriangular" | custom-call | tf_op jit(solution)/shard_map/jit(cholesky)/cholesky | solution.py:29
  258.0 1.2 constant_dynamic-update-slice_fusion.3
  259.2 1.1 convolution_subtract_fusion.5
  260.3 11.7 custom-call.21
  273.6 80.1 %custom-call.22 = f32[4,2,128,128]{2,3,1,0:T(8,128)} custom-call(f32[4,2,128,128]{3,2,1,0:T(8,128)} %pad_maximum_fusion), custom_call_target="InvertDiagBlocksLowerTriangular" | custom-call | tf_op jit(solution)/shard_map/vmap(jit(_cho_solve))/triangular_solve | solution.py:14
  353.7 2.0 fusion.116
  358.6 1.1 fusion.22
  359.7 3.3 convolution_bitcast_fusion.1
  363.0 155.4 %psum.14 = f32[4,320]{1,0:T(4,128)S(1)} all-reduce(f32[4,320]{1,0:T(4,128)S(1)} %convolution_bitcast_fusion.1), channel_id=1, replica_groups=mesh['chol'=64,'pop'=8] {'chol'}, use_global_device_ids=true, to_apply=%region_4.7 | all-reduce | flops 1280 | bytes 10240 | tf_op jit(solution)/shard_map/psum | solution.py:44
  518.4 8.1 copy.134
  526.5 3.8 fusion
  530.6 160.0 %all_gather.28 = bf16[4,640,160]{2,0,1:T(4,128)(2,1)S(1)} all-gather(bf16[4,10,160]{2,0,1:T(4,128)(2,1)S(1)} %copy.136), channel_id=1, replica_groups=mesh['chol'=64,'pop'=8] {'chol'}, dimensions={1}, use_global_device_ids=true | all-gather | bytes 832000 | tf_op jit(solution)/shard_map/all_gather | solution.py:63
  690.9 159.3 %all_gather.29 = bf16[4,640,160]{2,0,1:T(4,128)(2,1)S(1)} all-gather(bf16[4,10,160]{2,0,1:T(4,128)(2,1)S(1)} %copy.138), channel_id=1, replica_groups=mesh['chol'=64,'pop'=8] {'chol'}, dimensions={1}, use_global_device_ids=true | all-gather | bytes 832000 | tf_op jit(solution)/shard_map/all_gather | solution.py:63
  850.6 160.1 %all_gather.30 = bf16[4,640,160]{2,0,1:T(4,128)(2,1)S(1)} all-gather(bf16[4,10,160]{2,0,1:T(4,128)(2,1)S(1)} %copy.140), channel_id=1, replica_groups=mesh['chol'=64,'pop'=8] {'chol'}, dimensions={1}, use_global_device_ids=true | all-gather | bytes 832000 | tf_op jit(solution)/shard_map/all_gather | solution.py:63
  1011.0 158.1 %all_gather.31 = bf16[4,640,160]{2,0,1:T(4,128)(2,1)S(1)} all-gather(bf16[4,10,160]{2,0,1:T(4,128)(2,1)S(1)} %copy.142), channel_id=1, replica_groups=mesh['chol'=64,'pop'=8] {'chol'}, dimensions={1}, use_global_device_ids=true | all-gather | bytes 832000 | tf_op jit(solution)/shard_map/all_gather | solution.py:25
  1171.1 47.1 %custom-call.23 = f32[4,128,128]{2,1,0:T(8,128)S(1)} custom-call(f32[4,128,128]{2,1,0:T(8,128)S(1)} %cholesky.218), custom_call_target="Cholesky" | custom-call | tf_op jit(solution)/shard_map/jit(cholesky)/cholesky | solution.py:29
  1218.3 39.3 %custom-call.24 = f32[4,1,128,128]{2,3,1,0:T(8,128)S(1)} custom-call(f32[4,1,128,128]{3,2,1,0:T(8,128)S(1)} %get-tuple-element.31), custom_call_target="InvertDiagBlocksLowerTriangular" | custom-call | tf_op jit(solution)/shard_map/jit(cholesky)/cholesky | solution.py:29
  1257.6 1.2 constant_dynamic-update-slice_fusion.1
  1258.8 1.1 convolution_subtract_fusion.4
  1259.9 11.7 custom-call.25
  1273.0 80.0 %custom-call.26 = f32[4,2,128,128]{2,3,1,0:T(8,128)} custom-call(f32[4,2,128,128]{3,2,1,0:T(8,128)} %pad_maximum_fusion.1), custom_call_target="InvertDiagBlocksLowerTriangular" | custom-call | tf_op jit(solution)/shard_map/vmap(jit(_cho_solve))/triangular_solve | solution.py:14
  1353.1 2.0 fusion.114
  1358.0 1.1 fusion.25
  1359.1 3.3 convolution_bitcast_fusion
  1362.4 156.7 %psum.15 = f32[4,320]{1,0:T(4,128)S(1)} all-reduce(f32[4,320]{1,0:T(4,128)S(1)} %convolution_bitcast_fusion), channel_id=1, replica_groups=mesh['chol'=64,'pop'=8] {'chol'}, use_global_device_ids=true, to_apply=%region_5.8 | all-reduce | flops 1280 | bytes 10240 | tf_op jit(solution)/shard_map/psum | solution.py:44
  1519.9 3.8 fusion.1
  1524.0 158.9 %all_gather.32 = bf16[4,640,160]{2,0,1:T(4,128)(2,1)S(1)} all-gather(bf16[4,10,160]{2,0,1:T(4,128)(2,1)S(1)} %copy.156), channel_id=1, replica_groups=mesh['chol'=64,'pop'=8] {'chol'}, dimensions={1}, use_global_device_ids=true | all-gather | bytes 832000 | tf_op jit(solution)/shard_map/all_gather | solution.py:63
  1683.3 158.5 %all_gather.33 = bf16[4,640,160]{2,0,1:T(4,128)(2,1)S(1)} all-gather(bf16[4,10,160]{2,0,1:T(4,128)(2,1)S(1)} %copy.158), channel_id=1, replica_groups=mesh['chol'=64,'pop'=8] {'chol'}, dimensions={1}, use_global_device_ids=true | all-gather | bytes 832000 | tf_op jit(solution)/shard_map/all_gather | solution.py:63
  1842.1 160.7 %all_gather.34 = bf16[4,640,160]{2,0,1:T(4,128)(2,1)S(1)} all-gather(bf16[4,10,160]{2,0,1:T(4,128)(2,1)S(1)} %copy.160), channel_id=1, replica_groups=mesh['chol'=64,'pop'=8] {'chol'}, dimensions={1}, use_global_device_ids=true | all-gather | bytes 832000 | tf_op jit(solution)/shard_map/all_gather | solution.py:63
  2003.1 299.3 %all_gather.35 = bf16[32,10,160]{2,1,0:T(8,128)(2,1)S(1)} all-gather(bf16[4,10,160]{2,1,0:T(8,128)(2,1)S(1)} %fusion.79), channel_id=1, replica_groups=mesh['chol'=64,'pop'=8] {'pop'}, dimensions={0}, use_global_device_ids=true | all-gather | bytes 115200 | tf_op jit(solution)/shard_map/all_gather | solution.py:69
  (89 shorter events, 16.7 us)
Async XLA Ops:
  170.8 0.8 copy-start
  353.6 2.8 copy-start.2
  518.4 8.1 copy-start.5
  850.3 160.4 %copy-start.4 = (bf16[4,10,160]{2,0,1:T(4,128)(2,1)S(1)}, bf16[4,10,160]{2,0,1:T(4,128)(2,1)}, u32[]{:S(2)}) copy-start(bf16[4,10,160]{2,0,1:T(4,128)(2,1)} %param.7) | copy-start | bytes 38404
  1170.2 0.8 copy-start.1
  1353.1 2.8 copy-start.3
  1842.1 460.3 %copy-start.6 = (s32[4]{0:T(128)S(1)}, s32[4]{0:T(128)}, u32[]{:S(2)}) copy-start(s32[4]{0:T(128)} %param.10) | copy-start | bytes 52
where the time goes:
time: 2300 us
  blocking collectives  1900 us (83%)
  other arithmetic  360 us (16%)
  matrix products  33.9 us (1%)
    all_gather x6, blocking collectives, local(): lax.all_gather(term_rows, 'chol', axis=1, tiled=True)  958 us
    all_gather x2, blocking collectives, local(): gathered = lax.all_gather(current, 'chol', axis=1, tiled=True)  327 us
    psum x2, blocking collectives, local(): bias_now = SQRT_DT * lax.psum(partial_bias, 'chol')  312 us
    all_gather x1, blocking collectives, local(): everyone = lax.all_gather(current, 'pop', axis=0, tiled=True)  299 us
    another operation x18, other arithmetic, local(): factor = jnp.linalg.cholesky(gram)  197 us
    another operation x11, other arithmetic, solve_each(): return jax.scipy.linalg.cho_solve((factor, True), target)  162 us

commit v1 on v0

v1 whole, which is shorter than its diff:
```python
import functools

import jax
import jax.numpy as jnp
from jax import lax
from jax.experimental import pallas as pl
from jax.experimental.pallas import tpu as pltpu
from jax.sharding import PartitionSpec as P

STEPS = 2
ORDER = 4
SQRT_DT = 0.1
MESH = pl.DeviceIdType.MESH
F32 = jnp.float32
BF16 = jnp.bfloat16
VMEM = pltpu.VMEM
ROWS = 10
PAD = 16
SIDE = 4
LIMIT = 48 * 1024 * 1024


def place():
    d = lax.axis_index("chol")
    return d // 16, (d // 4) % 4, d % 4


def chol_id(y, z, x):
    return {"chol": y * 16 + z * 4 + x}


def others(at):
    return [lax.rem(at + k, SIDE) for k in range(1, SIDE)]


def dot(a, b):
    return lax.dot_general(a, b, (((1,), (0,)), ((), ())), preferred_element_type=F32)


def dot_nt(a, b):
    return lax.dot_general(a, b, (((1,), (1,)), ((), ())), preferred_element_type=F32)


def split(a, parts):
    out = []
    for _ in range(parts):
        head = a.astype(BF16)
        out.append(head)
        a = a - head.astype(F32)
    return out


def greet(peers):
    barrier = pltpu.get_barrier_semaphore()
    for peer in peers:
        pl.semaphore_signal(barrier, inc=1, device_id=peer, device_id_type=MESH)
    pl.semaphore_wait(barrier, len(peers))


def push(src, dst, send, recv, peer):
    copy = pltpu.make_async_remote_copy(
        src_ref=src, dst_ref=dst, send_sem=send, recv_sem=recv, device_id=peer, device_id_type=MESH
    )
    copy.start()
    return copy


def spread(blocks, grid, sems, local_sem):
    send, recv = sems
    y, z, x = place()
    mine = pltpu.make_async_copy(blocks.at[z], grid.at[y, z, x], local_sem)
    mine.start()
    first = [
        push(blocks.at[w], grid.at[y, z, x], send.at[k], recv.at[k], chol_id(y, w, x))
        for k, w in enumerate(others(z))
    ]
    mine.wait()
    for copy in first:
        copy.wait()
    ys, xs = others(y), others(x)
    one, two = pl.ds(0, 2), pl.ds(2, 2)
    along_y = [
        push(grid.at[y, one, x], grid.at[y, one, x], send.at[3 + k], recv.at[3 + k], chol_id(b, z, x))
        for k, b in enumerate(ys)
    ]
    along_x = [
        push(grid.at[y, two, x], grid.at[y, two, x], send.at[6 + k], recv.at[6 + k], chol_id(y, z, b))
        for k, b in enumerate(xs)
    ]
    for copy in along_y:
        copy.wait()
    then_x = [
        push(grid.at[:, one, x], grid.at[:, one, x], send.at[9 + k], recv.at[9 + k], chol_id(y, z, b))
        for k, b in enumerate(xs)
    ]
    for copy in along_x:
        copy.wait()
    then_y = [
        push(grid.at[y, two, :], grid.at[y, two, :], send.at[12 + k], recv.at[12 + k], chol_id(b, z, x))
        for k, b in enumerate(ys)
    ]
    for copy in then_x + then_y:
        copy.wait()


def compact(grid, out, width):
    rows = lax.broadcasted_iota(jnp.int32, (8 * ROWS, 8 * PAD), 0)
    cols = lax.broadcasted_iota(jnp.int32, (8 * ROWS, 8 * PAD), 1)
    pick = (rows == (cols // PAD) * ROWS + cols % PAD) & (cols % PAD < ROWS)
    pick = jnp.where(pick, 1.0, 0.0).astype(BF16)
    for part in range(8):
        piece = grid[part // 2, 2 * (part % 2) : 2 * (part % 2) + 2].reshape(8 * PAD, grid.shape[-1])
        kept = dot(pick, piece).astype(BF16)
        out[8 * ROWS * part : 8 * ROWS * (part + 1), :] = kept[:, :width]


def cube_peers():
    y, z, x = place()
    return (
        [chol_id(y, b, x) for b in others(z)]
        + [chol_id(b, z, x) for b in others(y)]
        + [chol_id(y, z, b) for b in others(x)]
    )


def gather_kernel(blocks, phi, grid, send, recv, local_sem):
    greet(cube_peers())
    spread(blocks, grid, (send, recv), local_sem)
    compact(grid, phi, phi.shape[1])


def gather(blocks, occ):
    lanes = blocks.shape[2]
    return pl.pallas_call(
        gather_kernel,
        out_shape=jax.ShapeDtypeStruct((64 * ROWS, occ), BF16),
        in_specs=[pl.BlockSpec(memory_space=VMEM)],
        out_specs=pl.BlockSpec(memory_space=VMEM),
        scratch_shapes=[
            VMEM((SIDE, SIDE, SIDE, PAD, lanes), BF16),
            pltpu.SemaphoreType.DMA((15,)),
            pltpu.SemaphoreType.DMA((15,)),
            pltpu.SemaphoreType.DMA,
        ],
        compiler_params=pltpu.CompilerParams(collective_id=0, has_side_effects=True, vmem_limit_bytes=LIMIT),
        name="gather_walkers",
    )(blocks)


def theta_kernel(phi, out):
    orb, occ = phi.shape
    _, _, x = place()
    top = phi[:occ, :]
    rows = lax.broadcasted_iota(jnp.int32, (occ, occ), 0)
    cols = lax.broadcasted_iota(jnp.int32, (occ, occ), 1)
    eye = jnp.where(rows == cols, 1.0, 0.0).astype(F32)
    gram = dot_nt(top, top)
    scale = 1.0 / jnp.max(jnp.sum(jnp.abs(gram), axis=1, keepdims=True), axis=0, keepdims=True)
    start = top.astype(F32) * scale

    inv = 2.0 * start - dot((gram * (scale * scale)).astype(BF16), top)
    for _ in range(6):
        near = inv.astype(BF16)
        inv = 2.0 * inv - dot(dot_nt(near, top).astype(BF16), near)

    def miss_of(guess):
        return eye - sum(dot_nt(part, top) for part in split(guess, 3)[::-1])

    def size_of(miss):
        return jnp.sum(miss * miss)

    miss = miss_of(inv)
    size = size_of(miss)
    good = size < 0.5
    inv = jnp.where(good, inv, start)

    def more(state):
        count, size, _ = state
        return (count < 64) & jnp.logical_not(size < 1e-7)

    def refine(state):
        count, _, guess = state
        miss = miss_of(guess)
        m_hi, m_lo = split(miss, 2)
        g_hi, g_lo = split(guess, 2)
        guess = guess + (dot(m_lo, g_hi) + dot(m_hi, g_lo) + dot(m_hi, g_hi))
        return count + 1, size_of(miss), guess

    _, _, inv = lax.while_loop(more, refine, (0, jnp.float32(1.0), inv))

    sel_rows = lax.broadcasted_iota(jnp.int32, (SIDE * PAD, occ), 0)
    sel_cols = lax.broadcasted_iota(jnp.int32, (SIDE * PAD, occ), 1)
    r = sel_rows % PAD
    sel = (sel_cols == ((sel_rows // PAD) * SIDE + x) * ROWS + r) & (r < ROWS)
    sel = jnp.where(sel, 1.0, 0.0).astype(BF16)
    picked = [dot(sel, part).astype(BF16) for part in split(inv, 2)]
    theta = dot_nt(picked[1], phi[...]) + dot_nt(picked[0], phi[...])
    out[...] = theta.astype(BF16).reshape(SIDE, PAD, orb)


def theta_of(phi):
    orb, _ = phi.shape
    return pl.pallas_call(
        theta_kernel,
        out_shape=jax.ShapeDtypeStruct((SIDE, PAD, orb), BF16),
        in_specs=[pl.BlockSpec(memory_space=VMEM)],
        out_specs=pl.BlockSpec(memory_space=VMEM),
        compiler_params=pltpu.CompilerParams(vmem_limit_bytes=LIMIT),
        name="occupied_inverse_theta",
    )(phi)


def step_kernel(
    theta, chol_hbm, noise, phi, current, bias,
    chol, slab_theta, parts, total, blocks, grid, pot, send, recv, bias_send, bias_recv, local_sem, chol_sem,
):
    y, z, x = place()
    vecs, orb = chol.shape[1:]
    load = pltpu.make_async_copy(chol_hbm, chol, chol_sem)
    load.start()
    slab = z * SIDE + x

    barrier = pltpu.get_barrier_semaphore()

    @pl.when(y == 0)
    def _():
        plane = [lax.rem(slab + k, 16) for k in range(1, 16)]
        for peer in [{"chol": p} for p in plane] + [chol_id(b, z, x) for b in range(1, SIDE)]:
            pl.semaphore_signal(barrier, inc=1, device_id=peer, device_id_type=MESH)
        pl.semaphore_wait(barrier, 18)

        own = pltpu.make_async_copy(theta.at[z], slab_theta.at[z], local_sem)
        own.start()
        moves = [
            push(theta.at[b], slab_theta.at[z], send.at[k], recv.at[k], chol_id(0, b, x))
            for k, b in enumerate(others(z))
        ]
        own.wait()
        for move in moves:
            move.wait()
        load.wait()
        green = slab_theta[...].reshape(SIDE * PAD, orb)
        green_row = lax.broadcasted_iota(jnp.int32, green.shape, 0) % PAD

        def one_row(r, acc):
            return acc + dot_nt(jnp.where(green_row == r, green, jnp.zeros_like(green)), chol[r])

        acc = lax.fori_loop(0, ROWS, one_row, jnp.zeros((SIDE * PAD, vecs), F32))
        parts[slab] = jnp.sum(acc.reshape(SIDE, PAD, vecs), axis=1)
        moves = [
            push(parts.at[slab], parts.at[slab], bias_send.at[k], bias_recv.at[k], {"chol": p})
            for k, p in enumerate(plane)
        ]
        for move in moves:
            move.wait()
        total[...] = SQRT_DT * jnp.sum(parts[...], axis=0)
        moves = [
            push(total, total, bias_send.at[15 + k], bias_recv.at[15], chol_id(b + 1, z, x)) for k, b in enumerate(range(3))
        ]
        for move in moves:
            move.wait_send()

    @pl.when(y != 0)
    def _():
        for peer in cube_peers():
            pl.semaphore_signal(barrier, inc=1, device_id=peer, device_id_type=MESH)
        pl.semaphore_wait(barrier, 9)
        load.wait()
        pltpu.make_async_copy(total, total, bias_recv.at[15]).wait()

    bias[...] = total[...]
    field = (noise[...] - total[...]).astype(BF16).astype(F32)
    field = jnp.broadcast_to(field[:, None, :], (SIDE, PAD, vecs)).reshape(SIDE * PAD, vecs).astype(BF16)
    field_row = lax.broadcasted_iota(jnp.int32, field.shape, 0) % PAD

    def one_slab(r, acc):
        return acc + dot(jnp.where(field_row == r, field, jnp.zeros_like(field)), chol[r])

    acc = lax.fori_loop(0, ROWS, one_slab, jnp.zeros((SIDE * PAD, orb), F32))
    blocks[...] = (SQRT_DT * acc).astype(BF16).reshape(SIDE, PAD, orb)
    spread(blocks, grid, (send.at[pl.ds(3, 15)], recv.at[pl.ds(3, 15)]), local_sem)
    compact(grid, pot, orb)

    term = phi[...]
    sum_of = term.astype(F32)
    for order in range(1, ORDER + 1):
        term = (-dot(pot[...], term) / order).astype(BF16)
        sum_of = sum_of + term.astype(F32)
    current[...] = sum_of.astype(BF16)


def step(theta, chol, noise, phi):
    rows, vecs, orb = chol.shape
    occ = phi.shape[1]
    dma = pltpu.SemaphoreType.DMA
    vmem = pl.BlockSpec(memory_space=VMEM)
    return pl.pallas_call(
        step_kernel,
        out_shape=(
            jax.ShapeDtypeStruct((orb, occ), BF16),
            jax.ShapeDtypeStruct((SIDE, vecs), F32),
        ),
        in_specs=[vmem, pl.BlockSpec(memory_space=pl.ANY), vmem, vmem],
        out_specs=(vmem, vmem),
        scratch_shapes=[
            VMEM((rows, vecs, orb), BF16),
            VMEM((SIDE, PAD, orb), BF16),
            VMEM((16, SIDE, vecs), F32),
            VMEM((SIDE, vecs), F32),
            VMEM((SIDE, PAD, orb), BF16),
            VMEM((SIDE, SIDE, SIDE, PAD, orb), BF16),
            VMEM((orb, orb), BF16),
            dma((18,)),
            dma((18,)),
            dma((18,)),
            dma((16,)),
            dma,
            dma,
        ],
        compiler_params=pltpu.CompilerParams(collective_id=1, has_side_effects=True, vmem_limit_bytes=LIMIT),
        name="propagation_step",
    )(theta, chol, noise, phi)


def branch_kernel(sources, phi, out, blocks, everyone, send, recv, local_sem):
    y, z, x = place()
    pop = lax.axis_index("pop")
    pops = [lax.rem(pop + k, 8) for k in range(1, 8)]
    greet([chol_id(y, b, x) for b in others(z)] + [{"pop": p} for p in pops])
    orb, occ = phi.shape
    rows = lax.broadcasted_iota(jnp.int32, (SIDE * PAD, orb), 0)
    cols = lax.broadcasted_iota(jnp.int32, (SIDE * PAD, orb), 1)
    r = rows % PAD
    sel = (cols == (y * 16 + (rows // PAD) * SIDE + x) * ROWS + r) & (r < ROWS)
    picked = dot(jnp.where(sel, 1.0, 0.0).astype(BF16), phi[...]).astype(BF16)
    blocks[...] = picked.reshape(SIDE, PAD, occ)
    own = pltpu.make_async_copy(blocks.at[z], everyone.at[pop, z], local_sem)
    own.start()
    moves = [
        push(blocks.at[b], everyone.at[pop, z], send.at[k], recv.at[k], chol_id(y, b, x))
        for k, b in enumerate(others(z))
    ]
    own.wait()
    for move in moves:
        move.wait()
    moves = [
        push(everyone.at[pop], everyone.at[pop], send.at[3 + k], recv.at[3 + k], {"pop": p}) for k, p in enumerate(pops)
    ]
    for move in moves:
        move.wait()
    for slot in range(SIDE):
        source = sources[slot]
        out[slot] = everyone[source // SIDE, source % SIDE]


def branch(sources, phi):
    occ = phi.shape[1]
    dma = pltpu.SemaphoreType.DMA
    return pl.pallas_call(
        branch_kernel,
        out_shape=jax.ShapeDtypeStruct((SIDE, PAD, occ), BF16),
        in_specs=[pl.BlockSpec(memory_space=pltpu.SMEM), pl.BlockSpec(memory_space=VMEM)],
        out_specs=pl.BlockSpec(memory_space=VMEM),
        scratch_shapes=[
            VMEM((SIDE, PAD, occ), BF16),
            VMEM((8, SIDE, PAD, occ), BF16),
            dma((10,)),
            dma((10,)),
            dma,
        ],
        compiler_params=pltpu.CompilerParams(collective_id=2, has_side_effects=True, vmem_limit_bytes=LIMIT),
        name="branch_walkers",
    )(sources, phi)


def local(walkers, chol_vectors, noise, sources):
    _, row_count, occ = walkers.shape
    vec_count = chol_vectors.shape[0]
    chol = jnp.transpose(chol_vectors, (1, 0, 2))
    blocks = jnp.pad(walkers, ((0, 0), (0, PAD - row_count), (0, 256 - occ)))
    phi = gather(blocks, occ)
    biases = []
    for index in range(STEPS):
        phi, bias = step(theta_of(phi), chol, noise[index], phi)
        biases.append(bias)
    branched = branch(sources, phi)[:, :row_count, :]
    share = vec_count // lax.axis_size("chol")
    stacked = jnp.stack(biases)
    bias_share = lax.dynamic_slice_in_dim(stacked, lax.axis_index("chol") * share, share, 2)
    return branched, bias_share


def solution(mesh):
    return jax.shard_map(
        local,
        mesh=mesh,
        in_specs=(P("pop", "chol", None), P(None, "chol", None), P(None, "pop", None), P("pop")),
        out_specs=(P("pop", "chol", None), P(None, "pop", "chol")),
        check_vma=False,
    )
```

time: 2300 us -> 149 us (0.06)
  blocking collectives: 1900 us -> 0 us
  other arithmetic: 360 us -> 0.67 us
  Pallas kernels: 0 us -> 143 us
  matrix products: 33.9 us -> 0 us
    all_gather x9 -> x0, blocking collectives: 1580 us -> none  [the longest x6 958 us: local(): lax.all_gather(term_rows, 'chol', axis=1, tiled=True)]
    another operation x29 -> x0, other arithmetic: 359 us -> none  [the longest x18 197 us: local(): factor = jnp.linalg.cholesky(gram)]
    psum x2 -> x0, blocking collectives: 312 us -> none  [local(): bias_now = SQRT_DT * lax.psum(partial_bias, 'chol')]
    pallas_call x0 -> x6, Pallas kernels: none -> 143 us  [the longest x2 69.9 us: step(): pl.pallas_call(step_kernel, out_shape=(jax.ShapeDtypeStruct((orb, occ), B...]
where the time goes in v1:
time: 149 us
  Pallas kernels  143 us (96%)
  local copies, waits for them, and re-layouts  4.24 us (3%)
    pallas_call x2, Pallas kernels, step(): pl.pallas_call(step_kernel, out_shape=(jax.ShapeDtypeStruct((orb, occ), B...  69.9 us
    pallas_call x1, Pallas kernels, branch(): pl.pallas_call(branch_kernel, out_shape=jax.ShapeDtypeStruct((SIDE, PAD,...  42 us
    pallas_call x1, Pallas kernels, gather(): pl.pallas_call(gather_kernel, out_shape=jax.ShapeDtypeStruct((64 * ROWS,...  17.9 us
    pallas_call x2, Pallas kernels, theta_of(): pl.pallas_call(theta_kernel, out_shape=jax.ShapeDtypeStruct((SIDE, PAD, o...  13.5 us
    unnamed x8, local copies, waits for them, and re-layouts  3.52 us

profile of v1, /device:TPU:1, one launch (start us, length us, event | category | flops | bytes accessed | tf_op | source)
XLA Modules:
  0.0 148.9 jit_solution(13680890487661579571)
XLA Ops:
  0.6 0.7 copy.6
  1.4 17.9 %gather_walkers.1.phi = bf16[640,160]{1,0:T(8,128)(2,1)S(1)} custom-call(bf16[4,16,256]{2,1,0:T(8,128)(2,1)S(1)} %pad.4.blocks), custom_call_target="tpu_custom_call" | custom-call | tf_op jit(solution)/shard_map/gather_walkers/pallas_call | solution.py:134
  19.3 4.1 %occupied_inverse_theta.2.theta = bf16[4,16,640]{2,1,0:T(8,128)(2,1)S(1)} custom-call(bf16[640,160]{1,0:T(8,128)(2,1)S(1)} %gather_walkers.1.phi), custom_call_target="tpu_custom_call" | custom-call | tf_op jit(solution)/shard_map/occupied_inverse_theta/pallas_call | solution.py:203
  23.3 0.7 slice_bitcast_fusion
  24.1 0.0 copy-start
  24.1 2.2 %copy-done = bf16[320,10,640]{2,0,1:T(8,128)(2,1)S(1)} copy-done((bf16[320,10,640]{2,0,1:T(8,128)(2,1)S(1)}, bf16[320,10,640]{2,0,1:T(8,128)(2,1)}, u32[]{:S(2)}) %copy-start) | copy-done | bytes 4096024
  26.2 0.0 copy-start.1
  26.2 0.0 copy-start.2
  26.2 35.8 %propagation_step.2 = (bf16[640,160]{1,0:T(8,128)(2,1)S(1)}, f32[4,320]{1,0:T(4,128)S(1)}) custom-call(bf16[4,16,640]{2,1,0:T(8,128)(2,1)S(1)} %occupied_inverse_theta.2.theta, bf16[10,320,640]{2,1,0:T(8,128)(2,1)S(1)} %bitcast.8, f32[4,320]{1,0:T(4,128)S(1)} %get-tuple-element.13.noise, bf16[640,160]{1,0:T(8,128)(2,1)S(1)} %gather_walkers.1.phi), custom_call_target="tpu_custom_call" | custom-call | tf_op jit(solution)/shard_map/propagation_step/pallas_call | solution.py:297
  62.1 9.5 %occupied_inverse_theta.3.theta = bf16[4,16,640]{2,1,0:T(8,128)(2,1)S(1)} custom-call(bf16[640,160]{1,0:T(8,128)(2,1)S(1)} %get-tuple-element.6.phi), custom_call_target="tpu_custom_call" | custom-call | tf_op jit(solution)/shard_map/occupied_inverse_theta/pallas_call | solution.py:203
  71.5 0.0 copy-done.1
  71.5 34.0 %propagation_step.3 = (bf16[640,160]{1,0:T(8,128)(2,1)S(1)}, f32[4,320]{1,0:T(4,128)S(1)}) custom-call(bf16[4,16,640]{2,1,0:T(8,128)(2,1)S(1)} %occupied_inverse_theta.3.theta, bf16[10,320,640]{2,1,0:T(8,128)(2,1)S(1)} %bitcast.9, f32[4,320]{1,0:T(4,128)S(1)} %get-tuple-element.12.noise, bf16[640,160]{1,0:T(8,128)(2,1)S(1)} %get-tuple-element.6.phi), custom_call_target="tpu_custom_call" | custom-call | tf_op jit(solution)/shard_map/propagation_step/pallas_call | solution.py:297
  105.6 0.7 fusion
  106.3 0.0 copy-done.2
  106.3 42.0 %branch_walkers.1 = bf16[4,16,160]{2,1,0:T(8,128)(2,1)S(1)} custom-call(s32[4]{0:T(128)S(1)} %copy-done.2, bf16[640,160]{1,0:T(8,128)(2,1)S(1)} %get-tuple-element.7.phi), custom_call_target="tpu_custom_call" | custom-call | tf_op jit(solution)/shard_map/branch_walkers/pallas_call | solution.py:359
  148.3 0.6 copy.7
  (1 shorter events, 0.0 us)
Async XLA Ops:
  24.1 2.2 %copy-start = (bf16[320,10,640]{2,0,1:T(8,128)(2,1)S(1)}, bf16[320,10,640]{2,0,1:T(8,128)(2,1)}, u32[]{:S(2)}) copy-start(bf16[320,10,640]{2,0,1:T(8,128)(2,1)} %param.5) | copy-start | bytes 12288004
  26.2 45.3 %copy-start.1 = (bf16[320,10,640]{2,0,1:T(8,128)(2,1)S(1)}, bf16[320,10,640]{2,0,1:T(8,128)(2,1)}, u32[]{:S(2)}) copy-start(bf16[320,10,640]{2,0,1:T(8,128)(2,1)} %param.5) | copy-start | bytes 12288004
  26.2 80.0 %copy-start.2 = (s32[4]{0:T(128)S(1)}, s32[4]{0:T(128)}, u32[]{:S(2)}) copy-start(s32[4]{0:T(128)} %sources.1) | copy-start | bytes 52

commit v2 on v0

v2 whole, which is shorter than its diff:
```python
import jax
import jax.numpy as jnp
from jax import lax
from jax.experimental import pallas as pl
from jax.experimental.pallas import tpu as pltpu
from jax.sharding import PartitionSpec as P

STEPS = 2
ORDER = 4
SQRT_DT = 0.1
MESH = pl.DeviceIdType.MESH
F32 = jnp.float32
BF16 = jnp.bfloat16
VMEM = pltpu.VMEM
ROWS = 10
PAD = 16
SIDE = 4
MAIN = 512
LANES = 128
FLAG = 15
NEWTON = ((0.05, 5), (0.001, 8))
REFINE = 2
MISS = 1e-3
LIMIT = 60 * 1024 * 1024


def dot(a, b):
    return lax.dot_general(a, b, (((1,), (0,)), ((), ())), preferred_element_type=F32)


def dot_nt(a, b):
    return lax.dot_general(a, b, (((1,), (1,)), ((), ())), preferred_element_type=F32)


def split(a):
    head = a.astype(BF16)
    return head, (a - head.astype(F32)).astype(BF16)


def index(shape, axis):
    return lax.broadcasted_iota(jnp.int32, shape, axis)


def one_hot(mask):
    return jnp.where(mask, 1.0, 0.0).astype(BF16)


def chol_id(y, z, x):
    return {"chol": y * 16 + z * 4 + x}


def others(at):
    return [lax.rem(at + k, SIDE) for k in range(1, SIDE)]


def remote(src, dst, send, recv, peer):
    return pltpu.make_async_remote_copy(
        src_ref=src, dst_ref=dst, send_sem=send, recv_sem=recv, device_id=peer, device_id_type=MESH
    )


def start(copies):
    for copy in copies:
        copy.start()


def received(copies):
    for copy in copies:
        copy.wait_recv()


def sent(copies):
    for copy in copies:
        copy.wait_send()


def spread(at, blocks, grid, send, recv, local_sem):
    y, z, x = at
    ys, xs = others(y), others(x)
    one, two = pl.ds(0, 2), pl.ds(2, 2)

    def along(spot, axis, base):
        peers = [chol_id(b, z, x) for b in ys] if axis == 0 else [chol_id(y, z, b) for b in xs]
        return [remote(grid.at[spot], grid.at[spot], send.at[base + k], recv.at[base + k], p) for k, p in enumerate(peers)]

    mine = pltpu.make_async_copy(blocks.at[z], grid.at[y, z, x], local_sem)
    first = [
        remote(blocks.at[w], grid.at[y, z, x], send.at[k], recv.at[k], chol_id(y, w, x)) for k, w in enumerate(others(z))
    ]
    start(first)
    mine.start()
    mine.wait()
    received(first)
    along_y = along((y, one, x), 0, 3)
    along_x = along((y, two, x), 1, 6)
    start(along_y + along_x)
    received(along_y)
    then_x = along((slice(None), one, x), 1, 9)
    start(then_x)
    received(along_x)
    then_y = along((y, two, slice(None)), 0, 12)
    start(then_y)
    sent(first + along_y + along_x)
    received(then_x + then_y)
    return then_x + then_y


def eight(grid, part):
    return grid[part // 2, 2 * (part % 2) : 2 * (part % 2) + 2].reshape(8 * PAD, grid.shape[-1])


def pick_rows():
    shape = (8 * ROWS, 8 * PAD)
    row, col = index(shape, 0), index(shape, 1)
    same = row // ROWS == col // PAD
    return row % ROWS, col % PAD, same


def compact(grid, out):
    row, col, same = pick_rows()
    pick = one_hot(same & (row == col))
    for part in range(8):
        kept = dot(pick, eight(grid, part)).astype(BF16)
        out[8 * ROWS * part : 8 * ROWS * (part + 1), :] = kept


def compact_packed(grid, out):
    row, col, same = pick_rows()
    pick = one_hot(same & (row == col))
    rest = [one_hot(same & (col == ROWS + row // 4) & (row % 4 == s)) for s in range(4)]
    for part in range(8):
        piece = eight(grid, part)
        rows = pl.ds(8 * ROWS * part, 8 * ROWS)
        out[rows, :MAIN] = dot(pick, piece).astype(BF16)
        tail = sum(dot(rest[s], piece[:, LANES * s : LANES * (s + 1)]) for s in range(4))
        out[rows, MAIN:] = tail.astype(BF16)


def theta_rows(phi, out, x, tuned, products):
    orb, occ = phi.shape
    top = phi[:occ, :]
    gram = dot_nt(top, top)
    scale = 0.999 / jnp.max(jnp.sum(jnp.abs(gram), axis=1, keepdims=True), axis=0, keepdims=True)
    inv, square = top.astype(F32) * scale, gram * scale
    least = tuned
    for turn in range(products):
        c = 2.0 / (1.0 + least)
        least = 1.0 - ((1.0 - least) / (1.0 + least)) ** 2
        near = inv.astype(BF16)
        if turn > 0:
            square = dot_nt(near, top)
        inv = (2.0 * c) * inv - (c * c) * dot(square.astype(BF16), near)
    eye = jnp.where(index((occ, occ), 0) == index((occ, occ), 1), 1.0, 0.0)
    for _ in range(REFINE):
        head, rest = split(inv)
        miss = eye - (dot_nt(rest, top) + dot_nt(head, top))
        inv = inv + dot(miss.astype(BF16), head)
    size = jnp.sum(jnp.sum(miss * miss, axis=1, keepdims=True), axis=0, keepdims=True)

    shape = (SIDE * PAD, occ)
    row, col = index(shape, 0), index(shape, 1)
    sel = one_hot((col == (row // PAD * SIDE + x) * ROWS + row % PAD) & (row % PAD < ROWS))
    head, rest = [dot(sel, part).astype(BF16) for part in split(inv)]
    theta = dot_nt(rest, phi[...]) + dot_nt(head, phi[...])
    out[...] = theta.astype(BF16).reshape(SIDE, PAD, orb)
    return jnp.where(size < MISS, 0.0, 1.0)


def bias_rows(green, chol):
    rows, vecs, _ = chol.shape
    row = index(green.shape, 0) % PAD
    acc = sum(dot_nt(jnp.where(row == r, green, jnp.zeros_like(green)), chol[r]) for r in range(rows))
    return jnp.sum(acc.reshape(SIDE, PAD, vecs), axis=1)


def potential_blocks(field, chol, blocks):
    rows, vecs, _ = chol.shape
    field = field.astype(BF16).astype(F32)
    field = jnp.broadcast_to(field[:, None, :], (SIDE, PAD, vecs)).reshape(SIDE * PAD, vecs).astype(BF16)
    row = index(field.shape, 0) % PAD
    none = jnp.zeros_like(field)
    main = sum(dot(jnp.where(row == r, field, none), chol[r, :, :MAIN]) for r in range(rows))
    for s in range(4):
        tail = sum(dot(jnp.where(row == ROWS + r // 4, field, none), chol[r, :, MAIN:]) for r in range(s, rows, 4))
        lanes = slice(LANES * s, LANES * (s + 1))
        blocks[:, :, lanes] = (SQRT_DT * (main[:, lanes] + tail)).astype(BF16).reshape(SIDE, PAD, LANES)


def pack_walker(phi, blocks, y, x, missed):
    orb, occ = phi.shape
    shape = (SIDE * PAD, orb)
    row, col = index(shape, 0), index(shape, 1)
    base, r = (y * 16 + row // PAD * SIDE + x) * ROWS, row % PAD
    whole = dot(one_hot((col == base + r) & (r < ROWS)), phi[:, :LANES])
    rest = occ - LANES
    copies = dot(phi[:, LANES:], one_hot(index((rest, LANES), 0) == index((rest, LANES), 1) % rest)).astype(BF16)
    lane = index((SIDE * PAD, LANES), 1) // rest
    for s in range(4):
        at = 4 * (r - ROWS) + s
        tail = dot(one_hot((col == base + at) & (at >= 0) & (at < ROWS)), copies)
        whole = whole + jnp.where(lane == s, tail, 0.0)
    whole = jnp.where(index(whole.shape, 0) % PAD == FLAG, missed, whole)
    blocks[...] = whole.astype(BF16).reshape(SIDE, PAD, LANES)


def kernel(
    walkers, chol_hbm, noise, sources, out, bias, missed_out,
    chol, first_grid, phi, theta, slab_theta, parts, total, blocks, grid, pot, packed, everyone,
    send0, recv0, send, recv, bias_send, bias_recv, last_send, last_recv, local_sem, chol_sem,
):
    d, pop = lax.axis_index("chol"), lax.axis_index("pop")
    y, z, x = at = d // 16, (d // 4) % 4, d % 4
    slab = z * SIDE + x
    hi, core = pop // 2, pop % 2
    load = pltpu.make_async_copy(chol_hbm, chol, chol_sem)
    load.start()

    ring = []
    for k in range(1, 16):
        place = lax.rem(hi * 4 + z + k, 16)
        ring.append((place // 4, place % 4))
    twin = {"pop": hi * 2 + 1 - core}
    ring_peers = [{"chol": y * 16 + b * 4 + x, "pop": h * 2 + core} for h, b in ring]
    plane = [{"chol": lax.rem(slab + k, 16)} for k in range(1, 16)]
    y_peers = [chol_id(b, z, x) for b in others(y)]
    x_peers = [chol_id(y, z, b) for b in others(x)]

    barrier = pltpu.get_barrier_semaphore()

    def greet(peers):
        for peer in peers:
            pl.semaphore_signal(barrier, inc=1, device_id=peer, device_id_type=MESH)

    greet(ring_peers + [twin] + y_peers + x_peers)

    @pl.when(y == 0)
    def _():
        greet([chol_id(0, b, c) for b in others(z) for c in others(x)])
        pl.semaphore_wait(barrier, 31)

    @pl.when(y != 0)
    def _():
        pl.semaphore_wait(barrier, 22)

    last = spread(at, walkers, first_grid, send0, recv0, local_sem)
    compact(first_grid, phi)
    sent(last)

    missed = jnp.zeros((1, 1), F32)
    for s in range(STEPS):
        tuned, products = NEWTON[s]
        missed = missed + theta_rows(phi, theta.at[s], x, tuned, products)

        to_slab = [
            remote(theta.at[s, b], slab_theta.at[s, z], send.at[s, k], recv.at[s, k], chol_id(0, b, x))
            for k, b in enumerate(others(z))
        ]
        to_plane = [
            remote(parts.at[s, slab], parts.at[s, slab], bias_send.at[s, k], bias_recv.at[s, k], p)
            for k, p in enumerate(plane)
        ]
        to_rows = [
            remote(total.at[s], total.at[s], bias_send.at[s, 15 + k], bias_recv.at[s, 15], chol_id(1 + k, z, x))
            for k in range(3)
        ]

        @pl.when(y == 0)
        def _():
            start(to_slab)
            own = pltpu.make_async_copy(theta.at[s, z], slab_theta.at[s, z], local_sem)
            own.start()
            own.wait()
            if s == 0:
                load.wait()
            received(to_slab)
            parts[s, slab] = bias_rows(slab_theta[s].reshape(SIDE * PAD, chol.shape[2]), chol)
            start(to_plane)
            received(to_plane)
            total[s] = SQRT_DT * jnp.sum(parts[s], axis=0)
            start(to_rows)

        @pl.when(y != 0)
        def _():
            if s == 0:
                load.wait()
            to_rows[0].wait_recv()

        bias[s] = total[s]
        potential_blocks(noise[s] - total[s], chol, blocks.at[s])

        @pl.when(y == 0)
        def _():
            sent(to_slab + to_plane + to_rows)

        last = spread(at, blocks.at[s], grid.at[s], send.at[s, pl.ds(3, 15)], recv.at[s, pl.ds(3, 15)], local_sem)
        compact_packed(grid.at[s], pot)
        sent(last)

        term = phi[...]
        sum_of = term.astype(F32)
        for order in range(1, ORDER + 1):
            term = (-dot(pot[...], term) / order).astype(BF16)
            sum_of = sum_of + term.astype(F32)
        phi[...] = sum_of.astype(BF16)

    pack_walker(phi, packed, y, x, missed)
    spot = everyone.at[hi, core, z]
    to_ring = [
        remote(packed.at[b], spot, last_send.at[k], last_recv.at[k], peer)
        for k, ((_, b), peer) in enumerate(zip(ring, ring_peers, strict=True))
    ]
    start(to_ring)
    own = pltpu.make_async_copy(packed.at[z], spot, local_sem)
    own.start()
    own.wait()
    received(to_ring)
    mine = everyone.at[:, core]
    to_twin = [remote(mine, mine, last_send.at[15], last_recv.at[15], twin)]
    start(to_twin)
    sent(to_ring)
    received(to_twin)

    chosen = []
    for slot in range(SIDE):
        source = sources[slot]
        chosen.append(everyone[source // 8, source // 4 % 2, source % 4])
    whole = jnp.concatenate(chosen, axis=0)
    out[:, :, :LANES] = whole.reshape(SIDE, PAD, LANES)
    rest = out.shape[2] - LANES
    shape = (SIDE * PAD, SIDE * PAD)
    row, col = index(shape, 0), index(shape, 1)
    r = row % PAD
    back = one_hot(index((LANES, rest), 0) % rest == index((LANES, rest), 1))
    lane = index((SIDE * PAD, LANES), 1) // rest
    tail = jnp.zeros((SIDE * PAD, LANES), F32)
    for s in range(4):
        pick = one_hot((row // PAD == col // PAD) & (col % PAD == ROWS + r // 4) & (r % 4 == s) & (r < ROWS))
        tail = tail + jnp.where(lane == s, dot(pick, whole), 0.0)
    out[:, :, LANES:] = dot(tail.astype(BF16), back).astype(BF16).reshape(SIDE, PAD, rest)
    flags = everyone[...].reshape(8 * SIDE, PAD, LANES).astype(F32)
    bad = jnp.where((index(flags.shape, 1) == FLAG) & jnp.logical_not(flags == 0.0), 1.0, 0.0)
    missed_out[...] = jnp.max(jnp.max(bad, axis=0), axis=0, keepdims=True)
    sent(to_twin)


def propagate(walkers, chol, noise, sources):
    rows, vecs, orb = chol.shape
    occ = walkers.shape[2]
    dma = pltpu.SemaphoreType.DMA
    vmem = pl.BlockSpec(memory_space=VMEM)
    return pl.pallas_call(
        kernel,
        out_shape=(
            jax.ShapeDtypeStruct((SIDE, PAD, occ), BF16),
            jax.ShapeDtypeStruct((STEPS, SIDE, vecs), F32),
            jax.ShapeDtypeStruct((1, LANES), F32),
        ),
        in_specs=[vmem, pl.BlockSpec(memory_space=pl.ANY), vmem, pl.BlockSpec(memory_space=pltpu.SMEM)],
        out_specs=(vmem, vmem, vmem),
        scratch_shapes=[
            VMEM((rows, vecs, orb), BF16),
            VMEM((SIDE, SIDE, SIDE, PAD, occ), BF16),
            VMEM((orb, occ), BF16),
            VMEM((STEPS, SIDE, PAD, orb), BF16),
            VMEM((STEPS, SIDE, PAD, orb), BF16),
            VMEM((STEPS, 16, SIDE, vecs), F32),
            VMEM((STEPS, SIDE, vecs), F32),
            VMEM((STEPS, SIDE, PAD, MAIN), BF16),
            VMEM((STEPS, SIDE, SIDE, SIDE, PAD, MAIN), BF16),
            VMEM((orb, orb), BF16),
            VMEM((SIDE, PAD, LANES), BF16),
            VMEM((SIDE, 2, SIDE, PAD, LANES), BF16),
            dma((15,)),
            dma((15,)),
            dma((STEPS, 18)),
            dma((STEPS, 18)),
            dma((STEPS, 18)),
            dma((STEPS, 16)),
            dma((16,)),
            dma((16,)),
            dma,
            dma,
        ],
        compiler_params=pltpu.CompilerParams(collective_id=0, has_side_effects=True, vmem_limit_bytes=LIMIT),
        name="propagate",
    )(walkers, chol, noise, sources)


def solve_each(factor, target):
    return jax.scipy.linalg.cho_solve((factor, True), target)


def by_cholesky(walkers, chol_vectors, noise, sources):
    walk_count, row_count, occ_count = walkers.shape
    vec_count, _, orb_count = chol_vectors.shape
    first_row = lax.axis_index("chol") * row_count
    flat_chol = chol_vectors.reshape(vec_count, row_count * orb_count)
    current = walkers
    biases = []
    for step_index in range(STEPS):
        gathered = lax.all_gather(current, "chol", axis=1, tiled=True)
        phi = gathered.astype(F32)
        top_plain = gathered[:, :occ_count, :]
        gram = jnp.einsum("wai,waj->wij", top_plain, top_plain, preferred_element_type=F32)
        factor = jnp.linalg.cholesky(gram)
        inverse = jax.vmap(solve_each)(factor, jnp.swapaxes(phi[:, :occ_count, :], 1, 2))
        inverse_wide = jnp.pad(inverse, ((0, 0), (0, 0), (0, orb_count - occ_count)))
        inverse_cols = lax.dynamic_slice_in_dim(inverse_wide, first_row, row_count, 2)
        theta_slab = jnp.einsum("wja,wai->wji", phi, inverse_cols, precision=lax.Precision.HIGHEST).astype(BF16)
        green = jnp.swapaxes(theta_slab, 1, 2).reshape(walk_count, row_count * orb_count)
        partial_bias = lax.dot_general(green, flat_chol, (((1,), (1,)), ((), ())), preferred_element_type=F32)
        bias_now = SQRT_DT * lax.psum(partial_bias, "chol")
        biases.append(bias_now)
        field = (noise[step_index] - bias_now).astype(BF16)
        potential = SQRT_DT * jnp.dot(field, flat_chol, preferred_element_type=F32)
        potential = potential.reshape(walk_count, row_count, orb_count).astype(BF16)
        total = current.astype(F32)
        term = current
        for order in range(1, ORDER + 1):
            whole = gathered if order == 1 else lax.all_gather(term, "chol", axis=1, tiled=True)
            product = jnp.einsum("wij,wjb->wib", potential, whole, preferred_element_type=F32)
            term = (-product / order).astype(BF16)
            total = total + term.astype(F32)
        current = total.astype(BF16)
    everyone = lax.all_gather(current, "pop", axis=0, tiled=True)
    return everyone[sources], jnp.stack(biases)


def local(walkers, chol_vectors, noise, sources):
    _, row_count, _ = walkers.shape
    vec_count = chol_vectors.shape[0]
    padded = jnp.pad(walkers, ((0, 0), (0, PAD - row_count), (0, 0)))
    branched, bias, missed = propagate(padded, jnp.transpose(chol_vectors, (1, 0, 2)), noise, sources)
    branched, bias = lax.cond(
        missed[0, 0] == 0.0,
        lambda: (branched[:, :row_count, :], bias),
        lambda: by_cholesky(walkers, chol_vectors, noise, sources),
    )
    share = vec_count // lax.axis_size("chol")
    bias_share = lax.dynamic_slice_in_dim(bias, lax.axis_index("chol") * share, share, 2)
    return branched, bias_share


def solution(mesh):
    return jax.shard_map(
        local,
        mesh=mesh,
        in_specs=(P("pop", "chol", None), P(None, "chol", None), P(None, "pop", None), P("pop")),
        out_specs=(P("pop", "chol", None), P(None, "pop", "chol")),
        check_vma=False,
    )
```

time: 2300 us -> 115 us (0.05)
  blocking collectives: 1900 us -> 0 us
  other arithmetic: 360 us -> 0 us
  Pallas kernels: 0 us -> 111 us
  matrix products: 33.9 us -> 0 us
    all_gather x9 -> x0, blocking collectives: 1580 us -> none  [the longest x6 958 us: local(): lax.all_gather(term_rows, 'chol', axis=1, tiled=True)]
    another operation x32 -> x0, other arithmetic: 360 us -> none  [the longest x18 197 us: local(): factor = jnp.linalg.cholesky(gram)]
    psum x2 -> x0, blocking collectives: 312 us -> none  [local(): bias_now = SQRT_DT * lax.psum(partial_bias, 'chol')]
    pallas_call x0 -> x1, Pallas kernels: none -> 111 us  [propagate(): pl.pallas_call(kernel, out_shape=(jax.ShapeDtypeStruct((SIDE, PAD, occ),...]
where the time goes in v2:
time: 115 us
  Pallas kernels  111 us (97%)
  local copies, waits for them, and re-layouts  2.05 us (2%)
  between operations  1.32 us (1%)
    pallas_call x1, Pallas kernels, propagate(): pl.pallas_call(kernel, out_shape=(jax.ShapeDtypeStruct((SIDE, PAD, occ),...  111 us

profile of v2, /device:TPU:1, one launch (start us, length us, event | category | flops | bytes accessed | tf_op | source)
XLA Modules:
  0.0 115.0 jit_solution(1522890748929728878)
XLA Ops:
  0.6 0.7 copy.173
  1.4 0.6 pad.21.walkers
  2.0 0.0 copy-start.4
  2.0 0.0 copy-start.5
  2.0 0.0 copy-start.7
  2.0 111.4 %propagate.1 = (bf16[4,16,160]{2,1,0:T(8,128)(2,1)S(1)}, f32[2,4,320]{2,1,0:T(4,128)S(1)}, f32[1,128]{1,0:T(1,128)}) custom-call(bf16[4,16,160]{2,1,0:T(8,128)(2,1)} %pad.21.walkers, bf16[10,320,640]{2,1,0:T(8,128)(2,1)} %bitcast.107, f32[2,4,320]{2,1,0:T(4,128)} %noise.1, s32[4]{0:T(128)} %sources.1), custom_call_target="tpu_custom_call" | custom-call | tf_op jit(solution)/shard_map/propagate/pallas_call | solution.py:351
  114.0 0.0 copy-done.4
  114.0 0.0 copy-done.5
  114.0 0.0 copy-done.7
  114.0 0.3 conditional.1
  114.3 0.0 copy-start.6
  114.3 0.7 constant_dynamic-slice_fusion
  115.0 0.0 copy-done.6
  (1 shorter events, 0.0 us)
Async XLA Ops:
  2.0 112.0 %copy-start.4 = (bf16[4,10,160]{2,0,1:T(4,128)(2,1)S(1)}, bf16[4,10,160]{2,0,1:T(4,128)(2,1)}, u32[]{:S(2)}) copy-start(bf16[4,10,160]{2,0,1:T(4,128)(2,1)} %param.9) | copy-start | bytes 38404
  2.0 112.0 %copy-start.5 = (f32[2,4,320]{2,1,0:T(4,128)S(1)}, f32[2,4,320]{2,1,0:T(4,128)}, u32[]{:S(2)}) copy-start(f32[2,4,320]{2,1,0:T(4,128)} %noise.1) | copy-start | bytes 30724
  2.0 112.0 %copy-start.7 = (s32[4]{0:T(128)S(1)}, s32[4]{0:T(128)}, u32[]{:S(2)}) copy-start(s32[4]{0:T(128)} %sources.1) | copy-start | bytes 52
  114.3 0.7 copy-start.6

commit v3 on v2

v3 whole, which is shorter than its diff:
```python
import jax
import jax.numpy as jnp
from jax import lax
from jax.experimental import pallas as pl
from jax.experimental.pallas import tpu as pltpu
from jax.sharding import PartitionSpec as P

STEPS = 2
ORDER = 4
SQRT_DT = 0.1
MESH = pl.DeviceIdType.MESH
F32 = jnp.float32
BF16 = jnp.bfloat16
VMEM = pltpu.VMEM
ROWS = 10
PAD = 16
SIDE = 4
HALF = 256
LANES = 128
FLAGS = 384
FLAG = 15
NEWTON = ((0.05, 5), (0.001, 8))
REFINE = 2
MISS = 1e-3
LIMIT = 60 * 1024 * 1024


def dot(a, b):
    return lax.dot_general(a, b, (((1,), (0,)), ((), ())), preferred_element_type=F32)


def dot_nt(a, b):
    return lax.dot_general(a, b, (((1,), (1,)), ((), ())), preferred_element_type=F32)


def split(a):
    head = a.astype(BF16)
    return head, (a - head.astype(F32)).astype(BF16)


def index(shape, axis):
    return lax.broadcasted_iota(jnp.int32, shape, axis)


def one_hot(mask):
    return jnp.where(mask, 1.0, 0.0).astype(BF16)


def chol_id(y, z, x):
    return {"chol": y * 16 + z * 4 + x}


def others(at):
    return [lax.rem(at + k, SIDE) for k in range(1, SIDE)]


def remote(src, dst, send, recv, peer):
    return pltpu.make_async_remote_copy(
        src_ref=src, dst_ref=dst, send_sem=send, recv_sem=recv, device_id=peer, device_id_type=MESH
    )


def start(copies):
    for copy in copies:
        copy.start()


def received(copies):
    for copy in copies:
        copy.wait_recv()


def sent(copies):
    for copy in copies:
        copy.wait_send()


def inverse_of(top, tuned, products):
    occ = top.shape[0]
    gram = dot_nt(top, top)
    scale = 0.999 / jnp.max(jnp.sum(jnp.abs(gram), axis=1, keepdims=True), axis=0, keepdims=True)
    inv, square = top.astype(F32) * scale, gram * scale
    least = tuned
    for turn in range(products):
        c = 2.0 / (1.0 + least)
        least = 1.0 - ((1.0 - least) / (1.0 + least)) ** 2
        near = inv.astype(BF16)
        if turn > 0:
            square = dot_nt(near, top)
        inv = (2.0 * c) * inv - (c * c) * dot(square.astype(BF16), near)
    eye = jnp.where(index((occ, occ), 0) == index((occ, occ), 1), 1.0, 0.0)
    for _ in range(REFINE):
        head, rest = split(inv)
        miss = eye - (dot_nt(rest, top) + dot_nt(head, top))
        inv = inv + dot(miss.astype(BF16), head)
    return inv, jnp.sum(jnp.sum(miss * miss, axis=1, keepdims=True), axis=0, keepdims=True)


def theta_rows(inv, phi_t, x):
    occ, orb = phi_t.shape
    shape = (SIDE * PAD, occ)
    row, col = index(shape, 0), index(shape, 1)
    sel = one_hot((col == (row // PAD * SIDE + x) * ROWS + row % PAD) & (row % PAD < ROWS))
    head, rest = [dot(sel, part).astype(BF16) for part in split(inv)]
    theta = dot(rest, phi_t[...]) + dot(head, phi_t[...])
    return theta.astype(BF16).reshape(SIDE, PAD, orb)


def eight(grid, part):
    return grid[part // 2, 2 * (part % 2) : 2 * (part % 2) + 2].reshape(8 * PAD, grid.shape[-1])


def pick_rows():
    shape = (8 * ROWS, 8 * PAD)
    row, col = index(shape, 0), index(shape, 1)
    return row % ROWS, col % PAD, row // ROWS == col // PAD


def compact(grid, out, these):
    row, col, same = pick_rows()
    pick = one_hot(same & (row == col))
    for part in these:
        out[8 * ROWS * part : 8 * ROWS * (part + 1), :] = dot(pick, eight(grid, part)).astype(BF16)


def compact_packed(grid, out, c):
    row, col, same = pick_rows()
    pick = one_hot(same & (row == col))
    rest = [one_hot(same & (col == ROWS + row // 4) & (row % 4 == 2 * c + e)) for e in range(2)]
    for part in range(8):
        piece = eight(grid, part)
        rows = pl.ds(8 * ROWS * part, 8 * ROWS)
        out[rows, HALF * c : HALF * (c + 1)] = dot(pick, piece).astype(BF16)
        tail = sum(dot(rest[e], piece[:, LANES * e : LANES * (e + 1)]) for e in range(2))
        if c > 0:
            tail = tail + out[rows, 2 * HALF :].astype(F32)
        out[rows, 2 * HALF :] = tail.astype(BF16)


def bias_rows(green, chol):
    rows, vecs, _ = chol.shape
    row = index(green.shape, 0) % PAD
    acc = sum(dot_nt(jnp.where(row == r, green, jnp.zeros_like(green)), chol[r]) for r in range(rows))
    return jnp.sum(acc.reshape(SIDE, PAD, vecs), axis=1)


def potential_chunk(field, chol, c):
    rows, vecs, _ = chol.shape
    field = jnp.broadcast_to(field[:, None, :], (SIDE, PAD, vecs)).reshape(SIDE * PAD, vecs).astype(BF16)
    row = index(field.shape, 0) % PAD
    none = jnp.zeros_like(field)
    lanes = slice(HALF * c, HALF * (c + 1))
    main = sum(dot(jnp.where(row == r, field, none), chol[r, :, lanes]) for r in range(rows))
    tails = [
        sum(dot(jnp.where(row == ROWS + r // 4, field, none), chol[r, :, 2 * HALF :]) for r in range(2 * c + e, rows, 4))
        for e in range(2)
    ]
    whole = SQRT_DT * (main + jnp.concatenate(tails, axis=1))
    return whole.astype(BF16).reshape(SIDE, PAD, HALF)


def pack_walker(phi_t, blocks, y, x, missed):
    occ, orb = phi_t.shape
    shape = (SIDE * PAD, orb)
    row, col = index(shape, 0), index(shape, 1)
    base, r = (y * 16 + row // PAD * SIDE + x) * ROWS, row % PAD
    whole = dot_nt(one_hot((col == base + r) & (r < ROWS)), phi_t[:LANES, :])
    rest = occ - LANES
    copies = jnp.concatenate([phi_t[LANES:, :]] * 4, axis=0)
    lane = index((SIDE * PAD, LANES), 1) // rest
    for s in range(4):
        at = 4 * (r - ROWS) + s
        tail = dot_nt(one_hot((col == base + at) & (at >= 0) & (at < ROWS)), copies)
        whole = whole + jnp.where(lane == s, tail, 0.0)
    whole = jnp.where(index(whole.shape, 0) % PAD == FLAG, missed, whole)
    blocks[...] = whole.astype(BF16).reshape(SIDE, PAD, LANES)


def kernel(
    walkers, chol_hbm, noise, sources, out, bias, missed_out,
    chol, padded, first_grid, phi, phi_t, theta, slab_theta, parts, halves, blocks, grid, pot, packed, everyone,
    send0, recv0, send, recv, bias_send, bias_recv, last_send, last_recv, chol_sem,
):
    d, pop = lax.axis_index("chol"), lax.axis_index("pop")
    y, z, x = d // 16, (d // 4) % 4, d % 4
    slab, pair = z * SIDE + x, x // 2
    near, far = x + 1 - 2 * (x % 2), lax.rem(x + 2, SIDE)
    hi, core = pop // 2, pop % 2
    load = pltpu.make_async_copy(chol_hbm, chol, chol_sem)
    load.start()

    ys, zs, xs = others(y), others(z), others(x)
    ring = []
    for k in range(1, 16):
        place = lax.rem(hi * 4 + z + k, 16)
        ring.append((place // 4, place % 4))
    twin = {"pop": hi * 2 + 1 - core}
    ring_peers = [{"chol": y * 16 + b * 4 + x, "pop": h * 2 + core} for h, b in ring]
    z_peers = [chol_id(y, b, x) for b in zs]
    y_peers = [chol_id(b, z, x) for b in ys]
    x_peers = [chol_id(y, z, b) for b in xs]
    barrier = pltpu.get_barrier_semaphore()

    def greet(peers):
        for peer in peers:
            pl.semaphore_signal(barrier, inc=1, device_id=peer, device_id_type=MESH)

    greet(ring_peers + x_peers + y_peers + [twin])

    @pl.when(y == 0)
    def _():
        greet([chol_id(0, b, near) for b in zs] + [chol_id(b, z, far) for b in range(1, SIDE)])

    @pl.when(y != 0)
    def _():
        greet([chol_id(0, z, far)])

    padded[...] = jnp.zeros_like(padded)
    padded[:, :ROWS, :] = walkers[...]

    @pl.when(y == 0)
    def _():
        pl.semaphore_wait(barrier, 28)

    @pl.when(y != 0)
    def _():
        pl.semaphore_wait(barrier, 23)

    def pushes(ref, spot, peers, sems, base):
        return [remote(ref.at[spot], ref.at[spot], sems[0].at[base + k], sems[1].at[base + k], p) for k, p in enumerate(peers)]

    one, two = pl.ds(0, 2), pl.ds(2, 2)
    sems0 = send0, recv0
    first = [
        remote(padded.at[w], first_grid.at[y, z, x], send0.at[k], recv0.at[k], peer)
        for k, (w, peer) in enumerate(zip(zs, z_peers, strict=True))
    ]
    start(first)
    first_grid[y, z, x] = padded[z]
    received(first)
    along_y = pushes(first_grid, (y, one, x), y_peers, sems0, 3)
    along_x = pushes(first_grid, (y, two, x), x_peers, sems0, 6)
    then_y = pushes(first_grid, (y, two, slice(None)), y_peers, sems0, 9)
    start(along_y + along_x)

    @pl.when(y != 0)
    def _():
        then_x = pushes(first_grid, (slice(None), one, x), x_peers, sems0, 12)
        received(along_y)
        start(then_x)
        received(along_x)
        start(then_y)
        sent(first + along_y + along_x)
        received(then_x + then_y)
        compact(first_grid, phi, range(8))
        sent(then_x + then_y)

    for s in range(STEPS):
        to_slab = [
            remote(theta.at[s, b], slab_theta.at[s, z], send.at[s, k], recv.at[s, k], peer)
            for k, (b, peer) in enumerate(zip(zs, z_peers, strict=True))
        ]
        pairs = [(lax.rem(z + k // 2, SIDE), (x, near)[k % 2]) for k in range(1, 8)]
        to_pair = [
            remote(parts.at[s, slab], parts.at[s, slab], bias_send.at[s, k], bias_recv.at[s, k], chol_id(0, b, c))
            for k, (b, c) in enumerate(pairs)
        ]
        half = halves.at[s, pair]
        to_rows = [
            remote(half, half, bias_send.at[s, 7 + k], bias_recv.at[s, 7 + pair], peer)
            for k, peer in enumerate([chol_id(b, z, c) for c in (x, far) for b in range(SIDE)][1:])
        ]

        def half_arrives(which, s=s):
            pltpu.make_async_copy(halves.at[s, which], halves.at[s, which], bias_recv.at[s, 7 + which]).wait()

        @pl.when(y == 0)
        def _(s=s):
            if s == 0:
                early = pushes(first_grid, (0, one, x), x_peers, sems0, 15)
                then_x = pushes(first_grid, (pl.ds(1, 3), one, x), x_peers, sems0, 12)
                start(early)
                received(along_y)
                start(then_x)
                received(along_x)
                start(then_y)
                received(early)
                compact(first_grid, phi, range(2))
                inv, size = inverse_of(phi[: phi.shape[1], :], *NEWTON[s])
                received(then_x + then_y)
                compact(first_grid, phi, range(2, 8))
                phi_t[...] = phi[...].astype(F32).T.astype(BF16)
            else:
                top = phi_t[:, : phi_t.shape[0]].astype(F32).T.astype(BF16)
                inv, size = inverse_of(top, *NEWTON[s])
            theta[s] = theta_rows(inv, phi_t, x)
            start(to_slab)
            slab_theta[s, z] = theta[s, z]
            if s == 0:
                sent(first + along_y + along_x + early + then_x + then_y)
                load.wait()
            missed = jnp.where(size < MISS, 0.0, 1.0)
            mine = parts.at[s, slab]
            mine[...] = jnp.zeros(mine.shape, F32)
            flags = index((SIDE, LANES), 0) == z
            mine[:, FLAGS:] = jnp.where(flags, missed, 0.0)
            received(to_slab)
            mine[:, : chol.shape[1]] = bias_rows(slab_theta[s].reshape(SIDE * PAD, chol.shape[2]), chol)
            start(to_pair)
            received(to_pair)
            half[...] = sum(parts[s, SIDE * b + 2 * pair + e] for e in range(2) for b in range(SIDE))
            start(to_rows)
            half_arrives(1 - pair)

        @pl.when(y != 0)
        def _(s=s):
            if s == 0:
                phi_t[...] = phi[...].astype(F32).T.astype(BF16)
                load.wait()
            half_arrives(0)
            half_arrives(1)

        total = halves[s, 0] + halves[s, 1]
        flag = jnp.sum(jnp.where(index((SIDE, LANES), 0) == z, total[:, FLAGS:], 0.0), axis=0, keepdims=True)[:, :1]
        missed = flag if s == 0 else missed + flag
        total = SQRT_DT * total[:, : chol.shape[1]]
        field = (noise[s] - total).astype(BF16).astype(F32)

        sems = send.at[s, pl.ds(3, 30)], recv.at[s, pl.ds(3, 30)]
        firsts, alongs, thens = [], [], []
        for c in range(2):
            blocks[s, c] = potential_chunk(field, chol, c)
            firsts.append([
                remote(blocks.at[s, c, w], grid.at[s, c, y, z, x], sems[0].at[15 * c + k], sems[1].at[15 * c + k], peer)
                for k, (w, peer) in enumerate(zip(zs, z_peers, strict=True))
            ])
            start(firsts[c])
            grid[s, c, y, z, x] = blocks[s, c, z]
        share = one_hot(index((chol.shape[1], 8), 0) == d * bias.shape[2] + index((chol.shape[1], 8), 1)).astype(F32)
        bias[s] = jnp.dot(total, share, precision=lax.Precision.HIGHEST, preferred_element_type=F32)[:, : bias.shape[2]]
        for c in range(2):
            received(firsts[c])
            view = grid.at[s, c]
            alongs.append((
                pushes(view, (y, one, x), y_peers, sems, 15 * c + 3),
                pushes(view, (y, two, x), x_peers, sems, 15 * c + 6),
            ))
            start(alongs[c][0] + alongs[c][1])
        for c in range(2):
            view = grid.at[s, c]
            then_x = pushes(view, (slice(None), one, x), x_peers, sems, 15 * c + 9)
            then_y = pushes(view, (y, two, slice(None)), y_peers, sems, 15 * c + 12)
            received(alongs[c][0])
            start(then_x)
            received(alongs[c][1])
            start(then_y)
            thens.append(then_x + then_y)
        for c in range(2):
            received(thens[c])
            compact_packed(grid.at[s, c], pot, c)

        term = phi_t[...]
        sum_of = term.astype(F32)
        for order in range(1, ORDER + 1):
            term = (-dot_nt(term, pot[...]) / order).astype(BF16)
            sum_of = sum_of + term.astype(F32)
        phi_t[...] = sum_of.astype(BF16)
        for c in range(2):
            sent(firsts[c] + alongs[c][0] + alongs[c][1] + thens[c])

        @pl.when(y == 0)
        def _():
            sent(to_slab + to_pair + to_rows)

    pack_walker(phi_t, packed, y, x, missed)
    spot = everyone.at[hi, core, z]
    to_ring = [
        remote(packed.at[b], spot, last_send.at[k], last_recv.at[k], peer)
        for k, ((_, b), peer) in enumerate(zip(ring, ring_peers, strict=True))
    ]
    start(to_ring)
    everyone[hi, core, z] = packed[z]
    received(to_ring)
    mine = everyone.at[:, core]
    to_twin = [remote(mine, mine, last_send.at[15], last_recv.at[15], twin)]
    start(to_twin)
    sent(to_ring)
    received(to_twin)

    chosen = []
    for slot in range(SIDE):
        source = sources[slot]
        chosen.append(everyone[source // 8, source // 4 % 2, source % 4])
    whole = jnp.concatenate(chosen, axis=0)
    out[:, :, :LANES] = whole.reshape(SIDE, PAD, LANES)
    rest = out.shape[2] - LANES
    shape = (SIDE * PAD, SIDE * PAD)
    row, col = index(shape, 0), index(shape, 1)
    r = row % PAD
    back = one_hot(index((LANES, rest), 0) % rest == index((LANES, rest), 1))
    lane = index((SIDE * PAD, LANES), 1) // rest
    tail = jnp.zeros((SIDE * PAD, LANES), F32)
    for s in range(4):
        pick = one_hot((row // PAD == col // PAD) & (col % PAD == ROWS + r // 4) & (r % 4 == s) & (r < ROWS))
        tail = tail + jnp.where(lane == s, dot(pick, whole), 0.0)
    out[:, :, LANES:] = dot(tail.astype(BF16), back).astype(BF16).reshape(SIDE, PAD, rest)
    flags = everyone[...].reshape(8 * SIDE, PAD, LANES).astype(F32)
    bad = jnp.where((index(flags.shape, 1) == FLAG) & jnp.logical_not(flags == 0.0), 1.0, 0.0)
    missed_out[...] = jnp.max(jnp.max(bad, axis=0), axis=0, keepdims=True)
    sent(to_twin)


def propagate(walkers, chol, noise, sources):
    rows, vecs, orb = chol.shape
    occ = walkers.shape[2]
    dma = pltpu.SemaphoreType.DMA
    vmem = pl.BlockSpec(memory_space=VMEM)
    return pl.pallas_call(
        kernel,
        out_shape=(
            jax.ShapeDtypeStruct((SIDE, PAD, occ), BF16),
            jax.ShapeDtypeStruct((STEPS, SIDE, vecs // SIDE**3), F32),
            jax.ShapeDtypeStruct((1, LANES), F32),
        ),
        in_specs=[vmem, pl.BlockSpec(memory_space=pl.ANY), vmem, pl.BlockSpec(memory_space=pltpu.SMEM)],
        out_specs=(vmem, vmem, vmem),
        scratch_shapes=[
            VMEM((rows, vecs, orb), BF16),
            VMEM((SIDE, PAD, occ), BF16),
            VMEM((SIDE, SIDE, SIDE, PAD, occ), BF16),
            VMEM((orb, occ), BF16),
            VMEM((occ, orb), BF16),
            VMEM((STEPS, SIDE, PAD, orb), BF16),
            VMEM((STEPS, SIDE, PAD, orb), BF16),
            VMEM((STEPS, 16, SIDE, FLAGS + LANES), F32),
            VMEM((STEPS, 2, SIDE, FLAGS + LANES), F32),
            VMEM((STEPS, 2, SIDE, PAD, HALF), BF16),
            VMEM((STEPS, 2, SIDE, SIDE, SIDE, PAD, HALF), BF16),
            VMEM((orb, orb), BF16),
            VMEM((SIDE, PAD, LANES), BF16),
            VMEM((SIDE, 2, SIDE, PAD, LANES), BF16),
            dma((18,)),
            dma((18,)),
            dma((STEPS, 33)),
            dma((STEPS, 33)),
            dma((STEPS, 14)),
            dma((STEPS, 9)),
            dma((16,)),
            dma((16,)),
            dma,
        ],
        compiler_params=pltpu.CompilerParams(collective_id=0, has_side_effects=True, vmem_limit_bytes=LIMIT),
        name="propagate",
    )(walkers, chol, noise, sources)


def solve_each(factor, target):
    return jax.scipy.linalg.cho_solve((factor, True), target)


def by_cholesky(walkers, chol_vectors, noise, sources):
    walk_count, row_count, occ_count = walkers.shape
    vec_count, _, orb_count = chol_vectors.shape
    first_row = lax.axis_index("chol") * row_count
    flat_chol = chol_vectors.reshape(vec_count, row_count * orb_count)
    current = walkers
    biases = []
    for step_index in range(STEPS):
        gathered = lax.all_gather(current, "chol", axis=1, tiled=True)
        phi = gathered.astype(F32)
        top_plain = gathered[:, :occ_count, :]
        gram = jnp.einsum("wai,waj->wij", top_plain, top_plain, preferred_element_type=F32)
        factor = jnp.linalg.cholesky(gram)
        inverse = jax.vmap(solve_each)(factor, jnp.swapaxes(phi[:, :occ_count, :], 1, 2))
        inverse_wide = jnp.pad(inverse, ((0, 0), (0, 0), (0, orb_count - occ_count)))
        inverse_cols = lax.dynamic_slice_in_dim(inverse_wide, first_row, row_count, 2)
        theta_slab = jnp.einsum("wja,wai->wji", phi, inverse_cols, precision=lax.Precision.HIGHEST).astype(BF16)
        green = jnp.swapaxes(theta_slab, 1, 2).reshape(walk_count, row_count * orb_count)
        partial_bias = lax.dot_general(green, flat_chol, (((1,), (1,)), ((), ())), preferred_element_type=F32)
        bias_now = SQRT_DT * lax.psum(partial_bias, "chol")
        biases.append(bias_now)
        field = (noise[step_index] - bias_now).astype(BF16)
        potential = SQRT_DT * jnp.dot(field, flat_chol, preferred_element_type=F32)
        potential = potential.reshape(walk_count, row_count, orb_count).astype(BF16)
        total = current.astype(F32)
        term = current
        for order in range(1, ORDER + 1):
            whole = gathered if order == 1 else lax.all_gather(term, "chol", axis=1, tiled=True)
            product = jnp.einsum("wij,wjb->wib", potential, whole, preferred_element_type=F32)
            term = (-product / order).astype(BF16)
            total = total + term.astype(F32)
        current = total.astype(BF16)
    everyone = lax.all_gather(current, "pop", axis=0, tiled=True)
    return everyone[sources], jnp.stack(biases)


def local(walkers, chol_vectors, noise, sources):
    _, row_count, _ = walkers.shape
    vec_count = chol_vectors.shape[0]
    share = vec_count // lax.axis_size("chol")
    branched, bias, missed = propagate(walkers, jnp.transpose(chol_vectors, (1, 0, 2)), noise, sources)

    def by_share():
        branched, bias = by_cholesky(walkers, chol_vectors, noise, sources)
        return branched, lax.dynamic_slice_in_dim(bias, lax.axis_index("chol") * share, share, 2)

    return lax.cond(missed[0, 0] == 0.0, lambda: (branched[:, :row_count, :], bias), by_share)


def solution(mesh):
    return jax.shard_map(
        local,
        mesh=mesh,
        in_specs=(P("pop", "chol", None), P(None, "chol", None), P(None, "pop", None), P("pop")),
        out_specs=(P("pop", "chol", None), P(None, "pop", "chol")),
        check_vma=False,
    )
```

time: 115 us -> 110 us (0.957)
  Pallas kernels: 111 us -> 106 us
    pallas_call x1, Pallas kernels: 111 us -> 106 us  [propagate(): pl.pallas_call(kernel, out_shape=(jax.ShapeDtypeStruct((SIDE, PAD, occ),...]
    unnamed x9 -> x10, local copies, waits for them, and re-layouts: 0.75 us -> 1.95 us
where the time goes in v3:
time: 110 us
  Pallas kernels  106 us (96%)
  local copies, waits for them, and re-layouts  1.96 us (2%)
  between operations  1.31 us (1%)
    pallas_call x1, Pallas kernels, propagate(): pl.pallas_call(kernel, out_shape=(jax.ShapeDtypeStruct((SIDE, PAD, occ),...  106 us

profile of v3, /device:TPU:1, one launch (start us, length us, event | category | flops | bytes accessed | tf_op | source)
XLA Modules:
  0.0 109.8 jit_solution(13512990729809845011)
XLA Ops:
  0.6 1.3 %copy.177.walkers = bf16[4,10,160]{2,1,0:T(8,128)(2,1)} copy(bf16[4,10,160]{2,0,1:T(4,128)(2,1)} %param.9) | data formatting | bytes 25600 | tf_op args[0]
  2.0 0.0 copy-start.4
  2.0 0.0 copy-start.5
  2.0 0.0 copy-start.7
  2.0 106.3 %propagate.1 = (bf16[4,16,160]{2,1,0:T(8,128)(2,1)S(1)}, f32[2,4,5]{2,1,0:T(4,128)S(1)}, f32[1,128]{1,0:T(1,128)}) custom-call(bf16[4,10,160]{2,1,0:T(8,128)(2,1)} %copy.177.walkers, bf16[10,320,640]{2,1,0:T(8,128)(2,1)} %bitcast.107, f32[2,4,320]{2,1,0:T(4,128)} %noise.1, s32[4]{0:T(128)} %sources.1), custom_call_target="tpu_custom_call" | custom-call | tf_op jit(solution)/shard_map/propagate/pallas_call | solution.py:418
  108.9 0.0 copy-done.4
  108.9 0.0 copy-done.5
  108.9 0.0 copy-done.7
  108.9 0.3 conditional.1
  109.2 0.0 copy-start.6
  109.2 0.6 copy.291
  109.8 0.0 copy-done.6
  (1 shorter events, 0.0 us)
Async XLA Ops:
  2.0 106.9 %copy-start.4 = (bf16[4,10,160]{2,0,1:T(4,128)(2,1)S(1)}, bf16[4,10,160]{2,0,1:T(4,128)(2,1)}, u32[]{:S(2)}) copy-start(bf16[4,10,160]{2,0,1:T(4,128)(2,1)} %param.9) | copy-start | bytes 38404
  2.0 106.9 %copy-start.5 = (f32[2,4,320]{2,1,0:T(4,128)S(1)}, f32[2,4,320]{2,1,0:T(4,128)}, u32[]{:S(2)}) copy-start(f32[2,4,320]{2,1,0:T(4,128)} %noise.1) | copy-start | bytes 30724
  2.0 106.9 %copy-start.7 = (s32[4]{0:T(128)S(1)}, s32[4]{0:T(128)}, u32[]{:S(2)}) copy-start(s32[4]{0:T(128)} %sources.1) | copy-start | bytes 52
  109.2 0.6 copy-start.6

commit v4 on v3

--- a/solution.py
+++ b/solution.py
@@ -106,8 +106,9 @@
     return theta.astype(BF16).reshape(SIDE, PAD, orb)
 
 
-def eight(grid, part):
-    return grid[part // 2, 2 * (part % 2) : 2 * (part % 2) + 2].reshape(8 * PAD, grid.shape[-1])
+def eight(block, part):
+    y, z = part // 2, 2 * (part % 2)
+    return jnp.concatenate([block(y, z + k // SIDE, k % SIDE) for k in range(8)], axis=0)
 
 
 def pick_rows():
@@ -116,19 +117,19 @@
     return row % ROWS, col % PAD, row // ROWS == col // PAD
 
 
-def compact(grid, out, these):
+def compact(block, out, these):
     row, col, same = pick_rows()
     pick = one_hot(same & (row == col))
     for part in these:
-        out[8 * ROWS * part : 8 * ROWS * (part + 1), :] = dot(pick, eight(grid, part)).astype(BF16)
-
-
-def compact_packed(grid, out, c):
+        out[8 * ROWS * part : 8 * ROWS * (part + 1), :] = dot(pick, eight(block, part)).astype(BF16)
+
+
+def compact_packed(block, out, c):
     row, col, same = pick_rows()
     pick = one_hot(same & (row == col))
     rest = [one_hot(same & (col == ROWS + row // 4) & (row % 4 == 2 * c + e)) for e in range(2)]
     for part in range(8):
-        piece = eight(grid, part)
+        piece = eight(block, part)
         rows = pl.ds(8 * ROWS * part, 8 * ROWS)
         out[rows, HALF * c : HALF * (c + 1)] = dot(pick, piece).astype(BF16)
         tail = sum(dot(rest[e], piece[:, LANES * e : LANES * (e + 1)]) for e in range(2))
@@ -216,7 +217,7 @@
         greet([chol_id(0, z, far)])
 
     padded[...] = jnp.zeros_like(padded)
-    padded[:, :ROWS, :] = walkers[...]
+    padded[:, :ROWS, :] = jnp.swapaxes(walkers[...].astype(F32), 0, 1).astype(BF16)
 
     @pl.when(y == 0)
     def _():
@@ -226,35 +227,41 @@
     def _():
         pl.semaphore_wait(barrier, 23)
 
-    def pushes(ref, spot, peers, sems, base):
-        return [remote(ref.at[spot], ref.at[spot], sems[0].at[base + k], sems[1].at[base + k], p) for k, p in enumerate(peers)]
-
-    one, two = pl.ds(0, 2), pl.ds(2, 2)
+    def pushes(ref, peers, sems, base):
+        return [remote(ref, ref, sems[0].at[base + k], sems[1].at[base + k], p) for k, p in enumerate(peers)]
+
     sems0 = send0, recv0
+    upper = z // 2
+    spot = first_grid.at[upper, x + upper * (y - x), y + upper * (x - y), z % 2]
     first = [
-        remote(padded.at[w], first_grid.at[y, z, x], send0.at[k], recv0.at[k], peer)
+        remote(padded.at[w], spot, send0.at[k], recv0.at[k], peer)
         for k, (w, peer) in enumerate(zip(zs, z_peers, strict=True))
     ]
     start(first)
-    first_grid[y, z, x] = padded[z]
+    spot[...] = padded[z]
     received(first)
-    along_y = pushes(first_grid, (y, one, x), y_peers, sems0, 3)
-    along_x = pushes(first_grid, (y, two, x), x_peers, sems0, 6)
-    then_y = pushes(first_grid, (y, two, slice(None)), y_peers, sems0, 9)
+    along_y = pushes(first_grid.at[0, x, y], y_peers, sems0, 3)
+    along_x = pushes(first_grid.at[1, y, x], x_peers, sems0, 6)
+    then_y = pushes(first_grid.at[1, y], y_peers, sems0, 9)
     start(along_y + along_x)
+
+    def first_block(b, c, e):
+        return first_grid[0, e, b, c] if c < 2 else first_grid[1, b, e, c - 2]
 
     @pl.when(y != 0)
     def _():
-        then_x = pushes(first_grid, (slice(None), one, x), x_peers, sems0, 12)
+        then_x = pushes(first_grid.at[0, x], x_peers, sems0, 12)
         received(along_y)
         start(then_x)
         received(along_x)
         start(then_y)
         sent(first + along_y + along_x)
         received(then_x + then_y)
-        compact(first_grid, phi, range(8))
+        compact(first_block, phi, range(8))
+        phi_t[...] = phi[...].astype(F32).T.astype(BF16)
         sent(then_x + then_y)
 
+    drain = []
     for s in range(STEPS):
         to_slab = [
             remote(theta.at[s, b], slab_theta.at[s, z], send.at[s, k], recv.at[s, k], peer)
@@ -275,20 +282,20 @@
             pltpu.make_async_copy(halves.at[s, which], halves.at[s, which], bias_recv.at[s, 7 + which]).wait()
 
         @pl.when(y == 0)
-        def _(s=s):
+        def _(s=s, drain=drain, led=led if s else []):
             if s == 0:
-                early = pushes(first_grid, (0, one, x), x_peers, sems0, 15)
-                then_x = pushes(first_grid, (pl.ds(1, 3), one, x), x_peers, sems0, 12)
+                early = pushes(first_grid.at[0, x, 0], x_peers, sems0, 15)
+                then_x = pushes(first_grid.at[0, x, pl.ds(1, 3)], x_peers, sems0, 12)
                 start(early)
                 received(along_y)
                 start(then_x)
                 received(along_x)
                 start(then_y)
                 received(early)
-                compact(first_grid, phi, range(2))
+                compact(first_block, phi, range(2))
                 inv, size = inverse_of(phi[: phi.shape[1], :], *NEWTON[s])
                 received(then_x + then_y)
-                compact(first_grid, phi, range(2, 8))
+                compact(first_block, phi, range(2, 8))
                 phi_t[...] = phi[...].astype(F32).T.astype(BF16)
             else:
                 top = phi_t[:, : phi_t.shape[0]].astype(F32).T.astype(BF16)
@@ -299,6 +306,7 @@
             if s == 0:
                 sent(first + along_y + along_x + early + then_x + then_y)
                 load.wait()
+            sent(drain + led)
             missed = jnp.where(size < MISS, 0.0, 1.0)
             mine = parts.at[s, slab]
             mine[...] = jnp.zeros(mine.shape, F32)
@@ -313,9 +321,9 @@
             half_arrives(1 - pair)
 
         @pl.when(y != 0)
-        def _(s=s):
+        def _(s=s, drain=drain):
+            sent(drain)
             if s == 0:
-                phi_t[...] = phi[...].astype(F32).T.astype(BF16)
                 load.wait()
             half_arrives(0)
             half_arrives(1)
@@ -326,38 +334,31 @@
         total = SQRT_DT * total[:, : chol.shape[1]]
         field = (noise[s] - total).astype(BF16).astype(F32)
 
-        sems = send.at[s, pl.ds(3, 30)], recv.at[s, pl.ds(3, 30)]
+        sems = send.at[s, pl.ds(3, 18)], recv.at[s, pl.ds(3, 18)]
         firsts, alongs, thens = [], [], []
-        for c in range(2):
+        for c, (u, v) in enumerate([(x, y), (y, x)]):
             blocks[s, c] = potential_chunk(field, chol, c)
+            spot = grid.at[s, c, u, v, z]
             firsts.append([
-                remote(blocks.at[s, c, w], grid.at[s, c, y, z, x], sems[0].at[15 * c + k], sems[1].at[15 * c + k], peer)
+                remote(blocks.at[s, c, w], spot, sems[0].at[9 * c + k], sems[1].at[9 * c + k], peer)
                 for k, (w, peer) in enumerate(zip(zs, z_peers, strict=True))
             ])
             start(firsts[c])
-            grid[s, c, y, z, x] = blocks[s, c, z]
+            spot[...] = blocks[s, c, z]
+        for c, (u, v, peers) in enumerate([(x, y, y_peers), (y, x, x_peers)]):
+            received(firsts[c])
+            alongs.append(pushes(grid.at[s, c, u, v], peers, sems, 9 * c + 3))
+            start(alongs[c])
+        for c, (u, peers) in enumerate([(x, x_peers), (y, y_peers)]):
+            received(alongs[c])
+            thens.append(pushes(grid.at[s, c, u], peers, sems, 9 * c + 6))
+            start(thens[c])
         share = one_hot(index((chol.shape[1], 8), 0) == d * bias.shape[2] + index((chol.shape[1], 8), 1)).astype(F32)
         bias[s] = jnp.dot(total, share, precision=lax.Precision.HIGHEST, preferred_element_type=F32)[:, : bias.shape[2]]
-        for c in range(2):
-            received(firsts[c])
-            view = grid.at[s, c]
-            alongs.append((
-                pushes(view, (y, one, x), y_peers, sems, 15 * c + 3),
-                pushes(view, (y, two, x), x_peers, sems, 15 * c + 6),
-            ))
-            start(alongs[c][0] + alongs[c][1])
-        for c in range(2):
-            view = grid.at[s, c]
-            then_x = pushes(view, (slice(None), one, x), x_peers, sems, 15 * c + 9)
-            then_y = pushes(view, (y, two, slice(None)), y_peers, sems, 15 * c + 12)
-            received(alongs[c][0])
-            start(then_x)
-            received(alongs[c][1])
-            start(then_y)
-            thens.append(then_x + then_y)
-        for c in range(2):
-            received(thens[c])
-            compact_packed(grid.at[s, c], pot, c)
+        received(thens[0])
+        compact_packed(lambda b, c, e, s=s: grid[s, 0, e, b, c], pot, 0)
+        received(thens[1])
+        compact_packed(lambda b, c, e, s=s: grid[s, 1, b, e, c], pot, 1)
 
         term = phi_t[...]
         sum_of = term.astype(F32)
@@ -365,12 +366,8 @@
             term = (-dot_nt(term, pot[...]) / order).astype(BF16)
             sum_of = sum_of + term.astype(F32)
         phi_t[...] = sum_of.astype(BF16)
-        for c in range(2):
-            sent(firsts[c] + alongs[c][0] + alongs[c][1] + thens[c])
-
-        @pl.when(y == 0)
-        def _():
-            sent(to_slab + to_pair + to_rows)
+        drain = sum(firsts + alongs + thens, [])
+        led = to_slab + to_pair + to_rows
 
     pack_walker(phi_t, packed, y, x, missed)
     spot = everyone.at[hi, core, z]
@@ -380,6 +377,12 @@
     ]
     start(to_ring)
     everyone[hi, core, z] = packed[z]
+    sent(drain)
+
+    @pl.when(y == 0)
+    def _():
+        sent(led)
+
     received(to_ring)
     mine = everyone.at[:, core]
     to_twin = [remote(mine, mine, last_send.at[15], last_recv.at[15], twin)]
@@ -392,7 +395,6 @@
         source = sources[slot]
         chosen.append(everyone[source // 8, source // 4 % 2, source % 4])
     whole = jnp.concatenate(chosen, axis=0)
-    out[:, :, :LANES] = whole.reshape(SIDE, PAD, LANES)
     rest = out.shape[2] - LANES
     shape = (SIDE * PAD, SIDE * PAD)
     row, col = index(shape, 0), index(shape, 1)
@@ -403,7 +405,9 @@
     for s in range(4):
         pick = one_hot((row // PAD == col // PAD) & (col % PAD == ROWS + r // 4) & (r % 4 == s) & (r < ROWS))
         tail = tail + jnp.where(lane == s, dot(pick, whole), 0.0)
-    out[:, :, LANES:] = dot(tail.astype(BF16), back).astype(BF16).reshape(SIDE, PAD, rest)
+    tail = dot(tail.astype(BF16), back)
+    whole = jnp.concatenate([whole.astype(F32), tail], axis=1).reshape(SIDE, PAD, LANES + rest)
+    out[...] = jnp.swapaxes(whole[:, :ROWS, :], 0, 1).astype(BF16)
     flags = everyone[...].reshape(8 * SIDE, PAD, LANES).astype(F32)
     bad = jnp.where((index(flags.shape, 1) == FLAG) & jnp.logical_not(flags == 0.0), 1.0, 0.0)
     missed_out[...] = jnp.max(jnp.max(bad, axis=0), axis=0, keepdims=True)
@@ -418,7 +422,7 @@
     return pl.pallas_call(
         kernel,
         out_shape=(
-            jax.ShapeDtypeStruct((SIDE, PAD, occ), BF16),
+            jax.ShapeDtypeStruct((rows, SIDE, occ), BF16),
             jax.ShapeDtypeStruct((STEPS, SIDE, vecs // SIDE**3), F32),
             jax.ShapeDtypeStruct((1, LANES), F32),
         ),
@@ -427,7 +431,7 @@
         scratch_shapes=[
             VMEM((rows, vecs, orb), BF16),
             VMEM((SIDE, PAD, occ), BF16),
-            VMEM((SIDE, SIDE, SIDE, PAD, occ), BF16),
+            VMEM((2, SIDE, SIDE, 2, PAD, occ), BF16),
             VMEM((orb, occ), BF16),
             VMEM((occ, orb), BF16),
             VMEM((STEPS, SIDE, PAD, orb), BF16),
@@ -441,8 +445,8 @@
             VMEM((SIDE, 2, SIDE, PAD, LANES), BF16),
             dma((18,)),
             dma((18,)),
-            dma((STEPS, 33)),
-            dma((STEPS, 33)),
+            dma((STEPS, 21)),
+            dma((STEPS, 21)),
             dma((STEPS, 14)),
             dma((STEPS, 9)),
             dma((16,)),
@@ -495,16 +499,17 @@
 
 
 def local(walkers, chol_vectors, noise, sources):
-    _, row_count, _ = walkers.shape
     vec_count = chol_vectors.shape[0]
     share = vec_count // lax.axis_size("chol")
-    branched, bias, missed = propagate(walkers, jnp.transpose(chol_vectors, (1, 0, 2)), noise, sources)
+    branched, bias, missed = propagate(
+        jnp.transpose(walkers, (1, 0, 2)), jnp.transpose(chol_vectors, (1, 0, 2)), noise, sources
+    )
 
     def by_share():
         branched, bias = by_cholesky(walkers, chol_vectors, noise, sources)
         return branched, lax.dynamic_slice_in_dim(bias, lax.axis_index("chol") * share, share, 2)
 
-    return lax.cond(missed[0, 0] == 0.0, lambda: (branched[:, :row_count, :], bias), by_share)
+    return lax.cond(missed[0, 0] == 0.0, lambda: (jnp.transpose(branched, (1, 0, 2)), bias), by_share)
 
 
 def solution(mesh):

time: 110 us -> 110 us (level)
  Pallas kernels: 106 us -> 108 us
  local copies, waits for them, and re-layouts: 1.96 us -> 0.64 us
    pallas_call x1, Pallas kernels: 106 us -> 108 us  [propagate(): pl.pallas_call(kernel, out_shape=(jax.ShapeDtypeStruct((rows, SIDE, occ),...]
    unnamed x10 -> x9, local copies, waits for them, and re-layouts: 1.95 us -> 0.62 us
where the time goes in v4:
time: 110 us
  Pallas kernels  108 us (98%)
  between operations  1.39 us (1%)
    pallas_call x1, Pallas kernels, propagate(): pl.pallas_call(kernel, out_shape=(jax.ShapeDtypeStruct((rows, SIDE, occ),...  108 us

profile of v4, /device:TPU:1, one launch (start us, length us, event | category | flops | bytes accessed | tf_op | source)
XLA Modules:
  0.0 109.9 jit_solution(9419882773517287880)
XLA Ops:
  0.6 0.0 copy-start.4
  0.6 0.0 copy-start.5
  0.6 0.0 copy-start.7
  0.7 107.6 %propagate.1 = (bf16[10,4,160]{2,1,0:T(4,128)(2,1)S(1)}, f32[2,4,5]{2,1,0:T(4,128)S(1)}, f32[1,128]{1,0:T(1,128)}) custom-call(bf16[10,4,160]{2,1,0:T(4,128)(2,1)} %bitcast.114, bf16[10,320,640]{2,1,0:T(8,128)(2,1)} %bitcast.110, f32[2,4,320]{2,1,0:T(4,128)} %noise.1, s32[4]{0:T(128)} %sources.1), custom_call_target="tpu_custom_call" | custom-call | tf_op jit(solution)/shard_map/propagate/pallas_call | solution.py:422
  109.0 0.0 copy-done.4
  109.0 0.0 copy-done.5
  109.0 0.0 copy-done.7
  109.0 0.3 conditional.1
  109.3 0.0 copy-start.6
  109.3 0.6 copy.293
  109.9 0.0 copy-done.6
  (2 shorter events, 0.0 us)
Async XLA Ops:
  0.6 108.4 %copy-start.4 = (bf16[4,10,160]{2,0,1:T(4,128)(2,1)S(1)}, bf16[4,10,160]{2,0,1:T(4,128)(2,1)}, u32[]{:S(2)}) copy-start(bf16[4,10,160]{2,0,1:T(4,128)(2,1)} %param.9) | copy-start | bytes 38404
  0.6 108.4 %copy-start.5 = (f32[2,4,320]{2,1,0:T(4,128)S(1)}, f32[2,4,320]{2,1,0:T(4,128)}, u32[]{:S(2)}) copy-start(f32[2,4,320]{2,1,0:T(4,128)} %noise.1) | copy-start | bytes 30724
  0.6 108.4 %copy-start.7 = (s32[4]{0:T(128)S(1)}, s32[4]{0:T(128)}, u32[]{:S(2)}) copy-start(s32[4]{0:T(128)} %sources.1) | copy-start | bytes 52
  109.3 0.6 copy-start.6

commit v5 on v4

--- a/solution.py
+++ b/solution.py
@@ -19,7 +19,7 @@
 LANES = 128
 FLAGS = 384
 FLAG = 15
-NEWTON = ((0.05, 5), (0.001, 8))
+NEWTON = ((0.05, 5), (0.001, 7))
 REFINE = 2
 MISS = 1e-3
 LIMIT = 60 * 1024 * 1024
@@ -160,27 +160,32 @@
     return whole.astype(BF16).reshape(SIDE, PAD, HALF)
 
 
-def pack_walker(phi_t, blocks, y, x, missed):
-    occ, orb = phi_t.shape
-    shape = (SIDE * PAD, orb)
+def pack_picks(picks, y, x):
+    shape = picks.shape[1:]
     row, col = index(shape, 0), index(shape, 1)
     base, r = (y * 16 + row // PAD * SIDE + x) * ROWS, row % PAD
-    whole = dot_nt(one_hot((col == base + r) & (r < ROWS)), phi_t[:LANES, :])
+    picks[0] = one_hot((col == base + r) & (r < ROWS))
+    for s in range(4):
+        at = 4 * (r - ROWS) + s
+        picks[1 + s] = one_hot((col == base + at) & (at >= 0) & (at < ROWS))
+
+
+def pack_walker(phi_t, picks, blocks, missed):
+    occ, _ = phi_t.shape
     rest = occ - LANES
+    whole = dot_nt(picks[0], phi_t[:LANES, :])
     copies = jnp.concatenate([phi_t[LANES:, :]] * 4, axis=0)
     lane = index((SIDE * PAD, LANES), 1) // rest
     for s in range(4):
-        at = 4 * (r - ROWS) + s
-        tail = dot_nt(one_hot((col == base + at) & (at >= 0) & (at < ROWS)), copies)
-        whole = whole + jnp.where(lane == s, tail, 0.0)
+        whole = whole + jnp.where(lane == s, dot_nt(picks[1 + s], copies), 0.0)
     whole = jnp.where(index(whole.shape, 0) % PAD == FLAG, missed, whole)
     blocks[...] = whole.astype(BF16).reshape(SIDE, PAD, LANES)
 
 
 def kernel(
     walkers, chol_hbm, noise, sources, out, bias, missed_out,
-    chol, padded, first_grid, phi, phi_t, theta, slab_theta, parts, halves, blocks, grid, pot, packed, everyone,
-    send0, recv0, send, recv, bias_send, bias_recv, last_send, last_recv, chol_sem,
+    chol, padded, first_grid, phi, phi_t, theta, slab_theta, parts, halves, blocks, grid, pot, picks, packed, everyone,
+    send0, recv0, send, recv, bias_send, bias_recv, last_send, last_recv, chol_sem, ready,
 ):
     d, pop = lax.axis_index("chol"), lax.axis_index("pop")
     y, z, x = d // 16, (d // 4) % 4, d % 4
@@ -206,26 +211,13 @@
         for peer in peers:
             pl.semaphore_signal(barrier, inc=1, device_id=peer, device_id_type=MESH)
 
-    greet(ring_peers + x_peers + y_peers + [twin])
-
-    @pl.when(y == 0)
-    def _():
-        greet([chol_id(0, b, near) for b in zs] + [chol_id(b, z, far) for b in range(1, SIDE)])
-
-    @pl.when(y != 0)
-    def _():
-        greet([chol_id(0, z, far)])
-
+    hi_peers = [{"pop": lax.rem(hi + k, 4) * 2 + core} for k in range(1, 4)]
+    lines = z_peers + x_peers + y_peers + hi_peers + [twin]
+    greet(lines)
     padded[...] = jnp.zeros_like(padded)
     padded[:, :ROWS, :] = jnp.swapaxes(walkers[...].astype(F32), 0, 1).astype(BF16)
 
-    @pl.when(y == 0)
-    def _():
-        pl.semaphore_wait(barrier, 28)
-
-    @pl.when(y != 0)
-    def _():
-        pl.semaphore_wait(barrier, 23)
+    pl.semaphore_wait(barrier, len(lines))
 
     def pushes(ref, peers, sems, base):
         return [remote(ref, ref, sems[0].at[base + k], sems[1].at[base + k], p) for k, p in enumerate(peers)]
@@ -244,6 +236,8 @@
     along_x = pushes(first_grid.at[1, y, x], x_peers, sems0, 6)
     then_y = pushes(first_grid.at[1, y], y_peers, sems0, 9)
     start(along_y + along_x)
+    for peer in hi_peers:
+        pl.semaphore_signal(ready, inc=1, device_id=peer, device_id_type=MESH)
 
     def first_block(b, c, e):
         return first_grid[0, e, b, c] if c < 2 else first_grid[1, b, e, c - 2]
@@ -306,6 +300,7 @@
             if s == 0:
                 sent(first + along_y + along_x + early + then_x + then_y)
                 load.wait()
+                pack_picks(picks, y, x)
             sent(drain + led)
             missed = jnp.where(size < MISS, 0.0, 1.0)
             mine = parts.at[s, slab]
@@ -325,6 +320,7 @@
             sent(drain)
             if s == 0:
                 load.wait()
+                pack_picks(picks, y, x)
             half_arrives(0)
             half_arrives(1)
 
@@ -369,7 +365,8 @@
         drain = sum(firsts + alongs + thens, [])
         led = to_slab + to_pair + to_rows
 
-    pack_walker(phi_t, packed, y, x, missed)
+    pl.semaphore_wait(ready, len(hi_peers))
+    pack_walker(phi_t, picks, packed, missed)
     spot = everyone.at[hi, core, z]
     to_ring = [
         remote(packed.at[b], spot, last_send.at[k], last_recv.at[k], peer)
@@ -441,6 +438,7 @@
             VMEM((STEPS, 2, SIDE, PAD, HALF), BF16),
             VMEM((STEPS, 2, SIDE, SIDE, SIDE, PAD, HALF), BF16),
             VMEM((orb, orb), BF16),
+            VMEM((5, SIDE * PAD, orb), BF16),
             VMEM((SIDE, PAD, LANES), BF16),
             VMEM((SIDE, 2, SIDE, PAD, LANES), BF16),
             dma((18,)),
@@ -452,6 +450,7 @@
             dma((16,)),
             dma((16,)),
             dma,
+            pltpu.SemaphoreType.REGULAR,
         ],
         compiler_params=pltpu.CompilerParams(collective_id=0, has_side_effects=True, vmem_limit_bytes=LIMIT),
         name="propagate",

time: 110 us -> 2410 us (21.91)
  blocking collectives: 0 us -> 1880 us
  other arithmetic: 0 us -> 360 us
  matrix products: 0 us -> 33 us
    all_gather x0 -> x9, blocking collectives: none -> 1570 us  [the longest x6 958 us: by_cholesky(): lax.all_gather(term, 'chol', axis=1, tiled=True)]
    another operation x0 -> x32, other arithmetic: none -> 360 us  [the longest x18 197 us: by_cholesky(): factor = jnp.linalg.cholesky(gram)]
    psum x0 -> x2, blocking collectives: none -> 312 us  [by_cholesky(): bias_now = SQRT_DT * lax.psum(partial_bias, 'chol')]
where the time goes in v5:
time: 2410 us; the launch traced here: 2400 us
  blocking collectives  1880 us (78%)
  other arithmetic  360 us (15%)
  Pallas kernels  107 us (4%)
  matrix products  33 us (1%)
    all_gather x6, blocking collectives, by_cholesky(): lax.all_gather(term, 'chol', axis=1, tiled=True)  958 us
    all_gather x2, blocking collectives, by_cholesky(): gathered = lax.all_gather(current, 'chol', axis=1, tiled=True)  319 us
    psum x2, blocking collectives, by_cholesky(): bias_now = SQRT_DT * lax.psum(partial_bias, 'chol')  312 us
    all_gather x1, blocking collectives, by_cholesky(): everyone = lax.all_gather(current, 'pop', axis=0, tiled=True)  294 us
    another operation x18, other arithmetic, by_cholesky(): factor = jnp.linalg.cholesky(gram)  197 us
    another operation x11, other arithmetic, solve_each(): return jax.scipy.linalg.cho_solve((factor, True), target)  163 us
    pallas_call x1, Pallas kernels, propagate(): pl.pallas_call(kernel, out_shape=(jax.ShapeDtypeStruct((rows, SIDE, occ),...  107 us

profile of v5, /device:TPU:1, one launch (start us, length us, event | category | flops | bytes accessed | tf_op | source)
XLA Modules:
  0.0 2400.4 jit_solution(11104417491789871836)
XLA Ops:
  0.7 107.5 %propagate.1 = (bf16[10,4,160]{2,1,0:T(4,128)(2,1)S(1)}, f32[2,4,5]{2,1,0:T(4,128)S(1)}, f32[1,128]{1,0:T(1,128)}) custom-call(bf16[10,4,160]{2,1,0:T(4,128)(2,1)} %bitcast.114, bf16[10,320,640]{2,1,0:T(8,128)(2,1)} %bitcast.110, f32[2,4,320]{2,1,0:T(4,128)} %noise.1, s32[4]{0:T(128)} %sources.1), custom_call_target="tpu_custom_call" | custom-call | tf_op jit(solution)/shard_map/propagate/pallas_call | solution.py:419
  108.9 2290.1 %conditional.1 = (f32[2,4,5]{2,1,0:T(4,128)S(1)}, bf16[4,10,160]{2,0,1:T(4,128)(2,1)S(1)}) conditional(s32[]{:T(128)} %bitcast.28, (bf16[4,10,160]{2,0,1:T(4,128)(2,1)S(1)}, f32[2,4,320]{2,1,0:T(4,128)S(1)}, bf16[320,10,640]{2,0,1:T(8,128)(2,1)}, s32[4]{0:T(128)S(1)}) %tuple.66, (bf16[10,4,160]{2,1,0:T(4,128)(2,1)S(1)}, ...), branch_computations={%region_0.9_spmd, %region_7.10_spmd} | conditional | flops 1021518656 | bytes 77151256 | solution.py:511
  108.9 161.0 %all_gather.18 = bf16[4,640,160]{2,0,1:T(4,128)(2,1)S(1)} all-gather(bf16[4,10,160]{2,0,1:T(4,128)(2,1)S(1)} %get-tuple-element.88), channel_id=1, replica_groups=mesh['chol'=64,'pop'=8] {'chol'}, dimensions={1}, use_global_device_ids=true | all-gather | bytes 832000 | tf_op jit(solution)/shard_map/cond/branch_0_fun/all_gather | solution.py:472
  271.8 46.9 %custom-call.19 = f32[4,128,128]{2,1,0:T(8,128)S(1)} custom-call(f32[4,128,128]{2,1,0:T(8,128)S(1)} %cholesky.215), custom_call_target="Cholesky" | custom-call | tf_op jit(solution)/shard_map/cond/branch_0_fun/jit(cholesky)/cholesky | solution.py:476
  318.8 39.3 %custom-call.20 = f32[4,1,128,128]{2,3,1,0:T(8,128)S(1)} custom-call(f32[4,1,128,128]{3,2,1,0:T(8,128)S(1)} %get-tuple-element.100), custom_call_target="InvertDiagBlocksLowerTriangular" | custom-call | tf_op jit(solution)/shard_map/cond/branch_0_fun/jit(cholesky)/cholesky | solution.py:476
  358.2 1.2 constant_dynamic-update-slice_fusion.3
  360.4 11.7 custom-call.21
  373.7 80.2 %custom-call.22 = f32[4,2,128,128]{2,3,1,0:T(8,128)} custom-call(f32[4,2,128,128]{3,2,1,0:T(8,128)} %pad_maximum_fusion), custom_call_target="InvertDiagBlocksLowerTriangular" | custom-call | tf_op jit(solution)/shard_map/cond/branch_0_fun/vmap(jit(_cho_solve))/triangular_solve | solution.py:461
  454.0 2.0 fusion.116
  458.9 1.1 fusion.22
  460.0 3.3 convolution_bitcast_fusion.1
  463.3 155.7 %psum.12 = f32[4,320]{1,0:T(4,128)S(1)} all-reduce(f32[4,320]{1,0:T(4,128)S(1)} %convolution_bitcast_fusion.1), channel_id=1, replica_groups=mesh['chol'=64,'pop'=8] {'chol'}, use_global_device_ids=true, to_apply=%region_5.7 | all-reduce | flops 1280 | bytes 10240 | tf_op jit(solution)/shard_map/cond/branch_0_fun/psum | solution.py:483
  619.1 8.1 copy.178
  627.1 3.8 fusion
  631.3 160.0 %all_gather.19 = bf16[4,640,160]{2,0,1:T(4,128)(2,1)S(1)} all-gather(bf16[4,10,160]{2,0,1:T(4,128)(2,1)S(1)} %copy.150), channel_id=1, replica_groups=mesh['chol'=64,'pop'=8] {'chol'}, dimensions={1}, use_global_device_ids=true | all-gather | bytes 832000 | tf_op jit(solution)/shard_map/cond/branch_0_fun/all_gather | solution.py:491
  791.6 158.4 %all_gather.20 = bf16[4,640,160]{2,0,1:T(4,128)(2,1)S(1)} all-gather(bf16[4,10,160]{2,0,1:T(4,128)(2,1)S(1)} %copy.152), channel_id=1, replica_groups=mesh['chol'=64,'pop'=8] {'chol'}, dimensions={1}, use_global_device_ids=true | all-gather | bytes 832000 | tf_op jit(solution)/shard_map/cond/branch_0_fun/all_gather | solution.py:491
  950.3 161.0 %all_gather.21 = bf16[4,640,160]{2,0,1:T(4,128)(2,1)S(1)} all-gather(bf16[4,10,160]{2,0,1:T(4,128)(2,1)S(1)} %copy.154), channel_id=1, replica_groups=mesh['chol'=64,'pop'=8] {'chol'}, dimensions={1}, use_global_device_ids=true | all-gather | bytes 832000 | tf_op jit(solution)/shard_map/cond/branch_0_fun/all_gather | solution.py:491
  1111.6 158.2 %all_gather.22 = bf16[4,640,160]{2,0,1:T(4,128)(2,1)S(1)} all-gather(bf16[4,10,160]{2,0,1:T(4,128)(2,1)S(1)} %copy.156), channel_id=1, replica_groups=mesh['chol'=64,'pop'=8] {'chol'}, dimensions={1}, use_global_device_ids=true | all-gather | bytes 832000 | tf_op jit(solution)/shard_map/cond/branch_0_fun/all_gather | solution.py:472
  1271.7 47.1 %custom-call.23 = f32[4,128,128]{2,1,0:T(8,128)S(1)} custom-call(f32[4,128,128]{2,1,0:T(8,128)S(1)} %cholesky.218), custom_call_target="Cholesky" | custom-call | tf_op jit(solution)/shard_map/cond/branch_0_fun/jit(cholesky)/cholesky | solution.py:476
  1319.0 39.3 %custom-call.24 = f32[4,1,128,128]{2,3,1,0:T(8,128)S(1)} custom-call(f32[4,1,128,128]{3,2,1,0:T(8,128)S(1)} %get-tuple-element.98), custom_call_target="InvertDiagBlocksLowerTriangular" | custom-call | tf_op jit(solution)/shard_map/cond/branch_0_fun/jit(cholesky)/cholesky | solution.py:476
  1358.3 1.2 constant_dynamic-update-slice_fusion.1
  1360.5 11.7 custom-call.25
  1373.7 80.3 %custom-call.26 = f32[4,2,128,128]{2,3,1,0:T(8,128)} custom-call(f32[4,2,128,128]{3,2,1,0:T(8,128)} %pad_maximum_fusion.1), custom_call_target="InvertDiagBlocksLowerTriangular" | custom-call | tf_op jit(solution)/shard_map/cond/branch_0_fun/vmap(jit(_cho_solve))/triangular_solve | solution.py:461
  1454.1 2.0 fusion.114
  1459.0 1.1 fusion.25
  1460.1 3.3 convolution_bitcast_fusion
  1463.4 156.4 %psum.13 = f32[4,320]{1,0:T(4,128)S(1)} all-reduce(f32[4,320]{1,0:T(4,128)S(1)} %convolution_bitcast_fusion), channel_id=1, replica_groups=mesh['chol'=64,'pop'=8] {'chol'}, use_global_device_ids=true, to_apply=%region_6.8 | all-reduce | flops 1280 | bytes 10240 | tf_op jit(solution)/shard_map/cond/branch_0_fun/psum | solution.py:483
  1619.9 3.8 fusion.1
  1624.0 159.1 %all_gather.23 = bf16[4,640,160]{2,0,1:T(4,128)(2,1)S(1)} all-gather(bf16[4,10,160]{2,0,1:T(4,128)(2,1)S(1)} %copy.171), channel_id=1, replica_groups=mesh['chol'=64,'pop'=8] {'chol'}, dimensions={1}, use_global_device_ids=true | all-gather | bytes 832000 | tf_op jit(solution)/shard_map/cond/branch_0_fun/all_gather | solution.py:491
  1783.4 159.5 %all_gather.24 = bf16[4,640,160]{2,0,1:T(4,128)(2,1)S(1)} all-gather(bf16[4,10,160]{2,0,1:T(4,128)(2,1)S(1)} %copy.173), channel_id=1, replica_groups=mesh['chol'=64,'pop'=8] {'chol'}, dimensions={1}, use_global_device_ids=true | all-gather | bytes 832000 | tf_op jit(solution)/shard_map/cond/branch_0_fun/all_gather | solution.py:491
  1943.2 160.4 %all_gather.25 = bf16[4,640,160]{2,0,1:T(4,128)(2,1)S(1)} all-gather(bf16[4,10,160]{2,0,1:T(4,128)(2,1)S(1)} %copy.175), channel_id=1, replica_groups=mesh['chol'=64,'pop'=8] {'chol'}, dimensions={1}, use_global_device_ids=true | all-gather | bytes 832000 | tf_op jit(solution)/shard_map/cond/branch_0_fun/all_gather | solution.py:491
  2103.9 294.1 %all_gather.26 = bf16[32,10,160]{2,1,0:T(8,128)(2,1)S(1)} all-gather(bf16[4,10,160]{2,1,0:T(8,128)(2,1)S(1)} %fusion.79), channel_id=1, replica_groups=mesh['chol'=64,'pop'=8] {'pop'}, dimensions={0}, use_global_device_ids=true | all-gather | bytes 115200 | tf_op jit(solution)/shard_map/cond/branch_0_fun/all_gather | solution.py:496
  (97 shorter events, 18.6 us)
Async XLA Ops:
  0.6 108.2 %copy-start.4 = (bf16[4,10,160]{2,0,1:T(4,128)(2,1)S(1)}, bf16[4,10,160]{2,0,1:T(4,128)(2,1)}, u32[]{:S(2)}) copy-start(bf16[4,10,160]{2,0,1:T(4,128)(2,1)} %param.9) | copy-start | bytes 38404
  0.6 108.2 %copy-start.5 = (f32[2,4,320]{2,1,0:T(4,128)S(1)}, f32[2,4,320]{2,1,0:T(4,128)}, u32[]{:S(2)}) copy-start(f32[2,4,320]{2,1,0:T(4,128)} %noise.1) | copy-start | bytes 30724
  0.6 108.2 %copy-start.7 = (s32[4]{0:T(128)S(1)}, s32[4]{0:T(128)}, u32[]{:S(2)}) copy-start(s32[4]{0:T(128)} %sources.1) | copy-start | bytes 52
  271.0 0.8 copy-start
  454.0 2.8 copy-start.2
  1270.8 0.8 copy-start.1
  1454.0 2.8 copy-start.3
  2399.0 0.6 copy-start.6

commit v6 on v5

--- a/solution.py
+++ b/solution.py
@@ -184,13 +184,11 @@
 
 def kernel(
     walkers, chol_hbm, noise, sources, out, bias, missed_out,
-    chol, padded, first_grid, phi, phi_t, theta, slab_theta, parts, halves, blocks, grid, pot, picks, packed, everyone,
+    chol, padded, first_grid, phi, phi_t, theta, slab_theta, parts, sums, blocks, grid, pot, picks, packed, everyone,
     send0, recv0, send, recv, bias_send, bias_recv, last_send, last_recv, chol_sem, ready,
 ):
     d, pop = lax.axis_index("chol"), lax.axis_index("pop")
     y, z, x = d // 16, (d // 4) % 4, d % 4
-    slab, pair = z * SIDE + x, x // 2
-    near, far = x + 1 - 2 * (x % 2), lax.rem(x + 2, SIDE)
     hi, core = pop // 2, pop % 2
     load = pltpu.make_async_copy(chol_hbm, chol, chol_sem)
     load.start()
@@ -261,19 +259,18 @@
             remote(theta.at[s, b], slab_theta.at[s, z], send.at[s, k], recv.at[s, k], peer)
             for k, (b, peer) in enumerate(zip(zs, z_peers, strict=True))
         ]
-        pairs = [(lax.rem(z + k // 2, SIDE), (x, near)[k % 2]) for k in range(1, 8)]
-        to_pair = [
-            remote(parts.at[s, slab], parts.at[s, slab], bias_send.at[s, k], bias_recv.at[s, k], chol_id(0, b, c))
-            for k, (b, c) in enumerate(pairs)
+        spots = [(k // SIDE, lax.rem(z + k % SIDE, SIDE)) for k in range(1, 16)]
+        to_sums = [
+            remote(parts.at[s, z], parts.at[s, z], bias_send.at[s, k], bias_recv.at[s, z], chol_id(b, c, x))
+            for k, (b, c) in enumerate(spots)
         ]
-        half = halves.at[s, pair]
-        to_rows = [
-            remote(half, half, bias_send.at[s, 7 + k], bias_recv.at[s, 7 + pair], peer)
-            for k, peer in enumerate([chol_id(b, z, c) for c in (x, far) for b in range(SIDE)][1:])
+        to_x = [
+            remote(sums.at[s, x], sums.at[s, x], bias_send.at[s, 15 + k], bias_recv.at[s, 4 + k], peer)
+            for k, peer in enumerate(x_peers)
         ]
 
-        def half_arrives(which, s=s):
-            pltpu.make_async_copy(halves.at[s, which], halves.at[s, which], bias_recv.at[s, 7 + which]).wait()
+        def part_arrives(which, s=s):
+            pltpu.make_async_copy(parts.at[s, which], parts.at[s, which], bias_recv.at[s, which]).wait()
 
         @pl.when(y == 0)
         def _(s=s, drain=drain, led=led if s else []):
@@ -303,17 +300,15 @@
                 pack_picks(picks, y, x)
             sent(drain + led)
             missed = jnp.where(size < MISS, 0.0, 1.0)
-            mine = parts.at[s, slab]
+            mine = parts.at[s, z]
             mine[...] = jnp.zeros(mine.shape, F32)
             flags = index((SIDE, LANES), 0) == z
             mine[:, FLAGS:] = jnp.where(flags, missed, 0.0)
             received(to_slab)
             mine[:, : chol.shape[1]] = bias_rows(slab_theta[s].reshape(SIDE * PAD, chol.shape[2]), chol)
-            start(to_pair)
-            received(to_pair)
-            half[...] = sum(parts[s, SIDE * b + 2 * pair + e] for e in range(2) for b in range(SIDE))
-            start(to_rows)
-            half_arrives(1 - pair)
+            start(to_sums)
+            for which in zs:
+                part_arrives(which)
 
         @pl.when(y != 0)
         def _(s=s, drain=drain):
@@ -321,10 +316,13 @@
             if s == 0:
                 load.wait()
                 pack_picks(picks, y, x)
-            half_arrives(0)
-            half_arrives(1)
-
-        total = halves[s, 0] + halves[s, 1]
+            for which in range(SIDE):
+                part_arrives(which)
+
+        sums[s, x] = sum(parts[s, which] for which in range(SIDE))
+        start(to_x)
+        received(to_x)
+        total = sum(sums[s, which] for which in range(SIDE))
         flag = jnp.sum(jnp.where(index((SIDE, LANES), 0) == z, total[:, FLAGS:], 0.0), axis=0, keepdims=True)[:, :1]
         missed = flag if s == 0 else missed + flag
         total = SQRT_DT * total[:, : chol.shape[1]]
@@ -362,8 +360,8 @@
             term = (-dot_nt(term, pot[...]) / order).astype(BF16)
             sum_of = sum_of + term.astype(F32)
         phi_t[...] = sum_of.astype(BF16)
-        drain = sum(firsts + alongs + thens, [])
-        led = to_slab + to_pair + to_rows
+        drain = sum(firsts + alongs + thens, to_x)
+        led = to_slab + to_sums
 
     pl.semaphore_wait(ready, len(hi_peers))
     pack_walker(phi_t, picks, packed, missed)
@@ -433,8 +431,8 @@
             VMEM((occ, orb), BF16),
             VMEM((STEPS, SIDE, PAD, orb), BF16),
             VMEM((STEPS, SIDE, PAD, orb), BF16),
-            VMEM((STEPS, 16, SIDE, FLAGS + LANES), F32),
-            VMEM((STEPS, 2, SIDE, FLAGS + LANES), F32),
+            VMEM((STEPS, SIDE, SIDE, FLAGS + LANES), F32),
+            VMEM((STEPS, SIDE, SIDE, FLAGS + LANES), F32),
             VMEM((STEPS, 2, SIDE, PAD, HALF), BF16),
             VMEM((STEPS, 2, SIDE, SIDE, SIDE, PAD, HALF), BF16),
             VMEM((orb, orb), BF16),
@@ -445,8 +443,8 @@
             dma((18,)),
             dma((STEPS, 21)),
             dma((STEPS, 21)),
-            dma((STEPS, 14)),
-            dma((STEPS, 9)),
+            dma((STEPS, 18)),
+            dma((STEPS, 7)),
             dma((16,)),
             dma((16,)),
             dma,

time: 2410 us -> 2410 us (level)
  no operation moved by 1% of the time
where the time goes in v6:
time: 2410 us; the launch traced here: 2400 us
  blocking collectives  1880 us (78%)
  other arithmetic  360 us (15%)
  Pallas kernels  107 us (4%)
  matrix products  33 us (1%)
    all_gather x6, blocking collectives, by_cholesky(): lax.all_gather(term, 'chol', axis=1, tiled=True)  958 us
    all_gather x2, blocking collectives, by_cholesky(): gathered = lax.all_gather(current, 'chol', axis=1, tiled=True)  320 us
    psum x2, blocking collectives, by_cholesky(): bias_now = SQRT_DT * lax.psum(partial_bias, 'chol')  311 us
    all_gather x1, blocking collectives, by_cholesky(): everyone = lax.all_gather(current, 'pop', axis=0, tiled=True)  293 us
    another operation x18, other arithmetic, by_cholesky(): factor = jnp.linalg.cholesky(gram)  197 us
    another operation x11, other arithmetic, solve_each(): return jax.scipy.linalg.cho_solve((factor, True), target)  163 us
    pallas_call x1, Pallas kernels, propagate(): pl.pallas_call(kernel, out_shape=(jax.ShapeDtypeStruct((rows, SIDE, occ),...  107 us

profile of v6, /device:TPU:1, one launch (start us, length us, event | category | flops | bytes accessed | tf_op | source)
XLA Modules:
  0.0 2399.1 jit_solution(13907885933308460423)
XLA Ops:
  0.7 106.9 %propagate.1 = (bf16[10,4,160]{2,1,0:T(4,128)(2,1)S(1)}, f32[2,4,5]{2,1,0:T(4,128)S(1)}, f32[1,128]{1,0:T(1,128)}) custom-call(bf16[10,4,160]{2,1,0:T(4,128)(2,1)} %bitcast.114, bf16[10,320,640]{2,1,0:T(8,128)(2,1)} %bitcast.110, f32[2,4,320]{2,1,0:T(4,128)} %noise.1, s32[4]{0:T(128)} %sources.1), custom_call_target="tpu_custom_call" | custom-call | tf_op jit(solution)/shard_map/propagate/pallas_call | solution.py:417
  108.3 2289.4 %conditional.1 = (f32[2,4,5]{2,1,0:T(4,128)S(1)}, bf16[4,10,160]{2,0,1:T(4,128)(2,1)S(1)}) conditional(s32[]{:T(128)} %bitcast.28, (bf16[4,10,160]{2,0,1:T(4,128)(2,1)S(1)}, f32[2,4,320]{2,1,0:T(4,128)S(1)}, bf16[320,10,640]{2,0,1:T(8,128)(2,1)}, s32[4]{0:T(128)S(1)}) %tuple.66, (bf16[10,4,160]{2,1,0:T(4,128)(2,1)S(1)}, ...), branch_computations={%region_0.9_spmd, %region_7.10_spmd} | conditional | flops 1021518656 | bytes 77151256 | solution.py:509
  108.3 160.8 %all_gather.18 = bf16[4,640,160]{2,0,1:T(4,128)(2,1)S(1)} all-gather(bf16[4,10,160]{2,0,1:T(4,128)(2,1)S(1)} %get-tuple-element.88), channel_id=1, replica_groups=mesh['chol'=64,'pop'=8] {'chol'}, dimensions={1}, use_global_device_ids=true | all-gather | bytes 832000 | tf_op jit(solution)/shard_map/cond/branch_0_fun/all_gather | solution.py:470
  271.1 46.9 %custom-call.19 = f32[4,128,128]{2,1,0:T(8,128)S(1)} custom-call(f32[4,128,128]{2,1,0:T(8,128)S(1)} %cholesky.215), custom_call_target="Cholesky" | custom-call | tf_op jit(solution)/shard_map/cond/branch_0_fun/jit(cholesky)/cholesky | solution.py:474
  318.1 39.3 %custom-call.20 = f32[4,1,128,128]{2,3,1,0:T(8,128)S(1)} custom-call(f32[4,1,128,128]{3,2,1,0:T(8,128)S(1)} %get-tuple-element.100), custom_call_target="InvertDiagBlocksLowerTriangular" | custom-call | tf_op jit(solution)/shard_map/cond/branch_0_fun/jit(cholesky)/cholesky | solution.py:474
  357.5 1.2 constant_dynamic-update-slice_fusion.3
  359.7 11.7 custom-call.21
  373.0 80.2 %custom-call.22 = f32[4,2,128,128]{2,3,1,0:T(8,128)} custom-call(f32[4,2,128,128]{3,2,1,0:T(8,128)} %pad_maximum_fusion), custom_call_target="InvertDiagBlocksLowerTriangular" | custom-call | tf_op jit(solution)/shard_map/cond/branch_0_fun/vmap(jit(_cho_solve))/triangular_solve | solution.py:459
  453.3 2.0 fusion.116
  458.2 1.1 fusion.22
  459.3 3.3 convolution_bitcast_fusion.1
  462.6 155.6 %psum.12 = f32[4,320]{1,0:T(4,128)S(1)} all-reduce(f32[4,320]{1,0:T(4,128)S(1)} %convolution_bitcast_fusion.1), channel_id=1, replica_groups=mesh['chol'=64,'pop'=8] {'chol'}, use_global_device_ids=true, to_apply=%region_5.7 | all-reduce | flops 1280 | bytes 10240 | tf_op jit(solution)/shard_map/cond/branch_0_fun/psum | solution.py:481
  618.3 8.1 copy.178
  626.3 3.8 fusion
  630.5 160.0 %all_gather.19 = bf16[4,640,160]{2,0,1:T(4,128)(2,1)S(1)} all-gather(bf16[4,10,160]{2,0,1:T(4,128)(2,1)S(1)} %copy.150), channel_id=1, replica_groups=mesh['chol'=64,'pop'=8] {'chol'}, dimensions={1}, use_global_device_ids=true | all-gather | bytes 832000 | tf_op jit(solution)/shard_map/cond/branch_0_fun/all_gather | solution.py:489
  790.7 159.3 %all_gather.20 = bf16[4,640,160]{2,0,1:T(4,128)(2,1)S(1)} all-gather(bf16[4,10,160]{2,0,1:T(4,128)(2,1)S(1)} %copy.152), channel_id=1, replica_groups=mesh['chol'=64,'pop'=8] {'chol'}, dimensions={1}, use_global_device_ids=true | all-gather | bytes 832000 | tf_op jit(solution)/shard_map/cond/branch_0_fun/all_gather | solution.py:489
  950.3 160.1 %all_gather.21 = bf16[4,640,160]{2,0,1:T(4,128)(2,1)S(1)} all-gather(bf16[4,10,160]{2,0,1:T(4,128)(2,1)S(1)} %copy.154), channel_id=1, replica_groups=mesh['chol'=64,'pop'=8] {'chol'}, dimensions={1}, use_global_device_ids=true | all-gather | bytes 832000 | tf_op jit(solution)/shard_map/cond/branch_0_fun/all_gather | solution.py:489
  1110.7 159.4 %all_gather.22 = bf16[4,640,160]{2,0,1:T(4,128)(2,1)S(1)} all-gather(bf16[4,10,160]{2,0,1:T(4,128)(2,1)S(1)} %copy.156), channel_id=1, replica_groups=mesh['chol'=64,'pop'=8] {'chol'}, dimensions={1}, use_global_device_ids=true | all-gather | bytes 832000 | tf_op jit(solution)/shard_map/cond/branch_0_fun/all_gather | solution.py:470
  1272.1 47.1 %custom-call.23 = f32[4,128,128]{2,1,0:T(8,128)S(1)} custom-call(f32[4,128,128]{2,1,0:T(8,128)S(1)} %cholesky.218), custom_call_target="Cholesky" | custom-call | tf_op jit(solution)/shard_map/cond/branch_0_fun/jit(cholesky)/cholesky | solution.py:474
  1319.4 39.3 %custom-call.24 = f32[4,1,128,128]{2,3,1,0:T(8,128)S(1)} custom-call(f32[4,1,128,128]{3,2,1,0:T(8,128)S(1)} %get-tuple-element.98), custom_call_target="InvertDiagBlocksLowerTriangular" | custom-call | tf_op jit(solution)/shard_map/cond/branch_0_fun/jit(cholesky)/cholesky | solution.py:474
  1358.7 1.2 constant_dynamic-update-slice_fusion.1
  1360.9 11.7 custom-call.25
  1374.1 80.3 %custom-call.26 = f32[4,2,128,128]{2,3,1,0:T(8,128)} custom-call(f32[4,2,128,128]{3,2,1,0:T(8,128)} %pad_maximum_fusion.1), custom_call_target="InvertDiagBlocksLowerTriangular" | custom-call | tf_op jit(solution)/shard_map/cond/branch_0_fun/vmap(jit(_cho_solve))/triangular_solve | solution.py:459
  1454.5 2.0 fusion.114
  1459.3 1.1 fusion.25
  1460.5 3.3 convolution_bitcast_fusion
  1463.8 155.5 %psum.13 = f32[4,320]{1,0:T(4,128)S(1)} all-reduce(f32[4,320]{1,0:T(4,128)S(1)} %convolution_bitcast_fusion), channel_id=1, replica_groups=mesh['chol'=64,'pop'=8] {'chol'}, use_global_device_ids=true, to_apply=%region_6.8 | all-reduce | flops 1280 | bytes 10240 | tf_op jit(solution)/shard_map/cond/branch_0_fun/psum | solution.py:481
  1619.3 3.8 fusion.1
  1623.4 159.7 %all_gather.23 = bf16[4,640,160]{2,0,1:T(4,128)(2,1)S(1)} all-gather(bf16[4,10,160]{2,0,1:T(4,128)(2,1)S(1)} %copy.171), channel_id=1, replica_groups=mesh['chol'=64,'pop'=8] {'chol'}, dimensions={1}, use_global_device_ids=true | all-gather | bytes 832000 | tf_op jit(solution)/shard_map/cond/branch_0_fun/all_gather | solution.py:489
  1783.4 159.4 %all_gather.24 = bf16[4,640,160]{2,0,1:T(4,128)(2,1)S(1)} all-gather(bf16[4,10,160]{2,0,1:T(4,128)(2,1)S(1)} %copy.173), channel_id=1, replica_groups=mesh['chol'=64,'pop'=8] {'chol'}, dimensions={1}, use_global_device_ids=true | all-gather | bytes 832000 | tf_op jit(solution)/shard_map/cond/branch_0_fun/all_gather | solution.py:489
  1943.1 159.9 %all_gather.25 = bf16[4,640,160]{2,0,1:T(4,128)(2,1)S(1)} all-gather(bf16[4,10,160]{2,0,1:T(4,128)(2,1)S(1)} %copy.175), channel_id=1, replica_groups=mesh['chol'=64,'pop'=8] {'chol'}, dimensions={1}, use_global_device_ids=true | all-gather | bytes 832000 | tf_op jit(solution)/shard_map/cond/branch_0_fun/all_gather | solution.py:489
  2103.3 293.4 %all_gather.26 = bf16[32,10,160]{2,1,0:T(8,128)(2,1)S(1)} all-gather(bf16[4,10,160]{2,1,0:T(8,128)(2,1)S(1)} %fusion.79), channel_id=1, replica_groups=mesh['chol'=64,'pop'=8] {'pop'}, dimensions={0}, use_global_device_ids=true | all-gather | bytes 115200 | tf_op jit(solution)/shard_map/cond/branch_0_fun/all_gather | solution.py:494
  (97 shorter events, 18.6 us)
Async XLA Ops:
  0.6 107.7 %copy-start.4 = (bf16[4,10,160]{2,0,1:T(4,128)(2,1)S(1)}, bf16[4,10,160]{2,0,1:T(4,128)(2,1)}, u32[]{:S(2)}) copy-start(bf16[4,10,160]{2,0,1:T(4,128)(2,1)} %param.9) | copy-start | bytes 38404
  0.6 107.7 %copy-start.5 = (f32[2,4,320]{2,1,0:T(4,128)S(1)}, f32[2,4,320]{2,1,0:T(4,128)}, u32[]{:S(2)}) copy-start(f32[2,4,320]{2,1,0:T(4,128)} %noise.1) | copy-start | bytes 30724
  0.6 107.7 %copy-start.7 = (s32[4]{0:T(128)S(1)}, s32[4]{0:T(128)}, u32[]{:S(2)}) copy-start(s32[4]{0:T(128)} %sources.1) | copy-start | bytes 52
  270.2 0.8 copy-start
  453.2 2.8 copy-start.2
  1271.2 0.8 copy-start.1
  1454.4 2.8 copy-start.3
  2397.7 0.6 copy-start.6
